TPU v7x, 32 devices: a whole 2x2x4 slice. The times are simulated.
32 devices in a mesh: replica: 4 (over x, core), fsdp: 8 (over z, y).
Axes of the slice: x: 2, y: 2, z: 4, core: 2. Of those that a mesh axis runs over, the one named last changes fastest.
Arguments:
- tokens: bfloat16 [32, 128, 768], P(('replica', 'fsdp')), may hold values from -6 to 6
- encoded: bfloat16 [32, 2, 64, 768], P(('replica', 'fsdp')), may hold values from -6 to 6
- lengths: int32 [32, 2], P(('replica', 'fsdp')), may hold values from 16 to 112, as said below
- cotangent: bfloat16 [32, 128, 768], P(('replica', 'fsdp')), may hold values from -6 to 6
- norm_self: bfloat16 [768], P('fsdp'), may hold values from 0.5 to 1.5
- q_self: bfloat16 [768, 768], P('fsdp'), may hold values from -0.109375 to 0.109375
- k_self: bfloat16 [768, 768], P('fsdp'), may hold values from -0.109375 to 0.109375
- v_self: bfloat16 [768, 768], P('fsdp'), may hold values from -0.21875 to 0.21875
- o_self: bfloat16 [768, 768], P('fsdp'), may hold values from -0.875 to 0.875
- bias_table: bfloat16 [32, 12], P('fsdp'), may hold values from -4 to 4
- norm_cross: bfloat16 [768], P('fsdp'), may hold values from 0.5 to 1.5
- q_cross: bfloat16 [768, 768], P('fsdp'), may hold values from -0.109375 to 0.109375
- k_cross: bfloat16 [768, 768], P('fsdp'), may hold values from -0.109375 to 0.109375
- v_cross: bfloat16 [768, 768], P('fsdp'), may hold values from -0.21875 to 0.21875
- o_cross: bfloat16 [768, 768], P('fsdp'), may hold values from -0.875 to 0.875
- norm_ff: bfloat16 [768], P('fsdp'), may hold values from 0.5 to 1.5
- wi_gate: bfloat16 [768, 2048], P('fsdp'), may hold values from -0.21875 to 0.21875
- wi_up: bfloat16 [768, 2048], P('fsdp'), may hold values from -0.21875 to 0.21875
- wo_ff: bfloat16 [2048, 768], P('fsdp'), may hold values from -0.125 to 0.125
Outputs:
- mixed: bfloat16 [32, 128, 768], P(('replica', 'fsdp'))
- tokens_grad: float32 [32, 128, 768], P(('replica', 'fsdp'))
- encoded_grad: float32 [32, 2, 64, 768], P(('replica', 'fsdp'))
- norm_self_grad: float32 [768], P('fsdp')
- q_self_grad: float32 [768, 768], P('fsdp')
- k_self_grad: float32 [768, 768], P('fsdp')
- v_self_grad: float32 [768, 768], P('fsdp')
- o_self_grad: float32 [768, 768], P('fsdp')
- bias_table_grad: float32 [32, 12], P('fsdp')
- norm_cross_grad: float32 [768], P('fsdp')
- q_cross_grad: float32 [768, 768], P('fsdp')
- k_cross_grad: float32 [768, 768], P('fsdp')
- v_cross_grad: float32 [768, 768], P('fsdp')
- o_cross_grad: float32 [768, 768], P('fsdp')
- norm_ff_grad: float32 [768], P('fsdp')
- wi_gate_grad: float32 [768, 2048], P('fsdp')
- wi_up_grad: float32 [768, 2048], P('fsdp')
- wo_ff_grad: float32 [2048, 768], P('fsdp')
Inputs may be any that keep to these rules, and one draw needn't show every extreme that they name: Each slot holds two sequences packed from its first row; their lengths sum to at most 128, and some slot is filled to 128 in every draw.
All inputs are finite; a program needn't handle non-finite values.
Results may differ from a plain program's by a relative error of at most 0.025.
The roundings to bfloat16 on the way count: a program that leaves them out, or rounds other values in their place, can miss the bound.
Values may be sent and summed in bfloat16 or wider, within the bound.
No kernel may reach another device: no remote copies, remote signals or barrier semaphores. Data moves between devices by JAX's collectives and lax.ppermute only.
A program may use at most 128 MiB of HBM per device.

v0:
```python
import functools
import math

import jax
import jax.numpy as jnp
import numpy as np
from jax import lax
from jax.experimental import pallas as pl
from jax.experimental.pallas import tpu as pltpu
from jax.sharding import PartitionSpec as P

HEADS = 12
PAIR = 128
EPS = 1e-06
NEG = -1e30
SQRT_2_PI = math.sqrt(2 / math.pi)
bucket_edges = np.array([math.ceil(16 * 8 ** (k / 16)) for k in range(1, 16)], np.int32)

F32 = jnp.float32
BF16 = jnp.bfloat16
VMEM = pl.BlockSpec(memory_space=pltpu.VMEM)
SMEM = pl.BlockSpec(memory_space=pltpu.SMEM)
ANY = pl.BlockSpec(memory_space=pl.ANY)


def params(limit=56):
    return pltpu.CompilerParams(vmem_limit_bytes=limit * 1024 * 1024)


def cost(flops, nbytes):
    return pl.CostEstimate(flops=flops, bytes_accessed=nbytes, transcendentals=0)


def bucket_of(offset):
    distance = jnp.maximum(offset, 0)
    counted = jnp.sum((distance[..., None] >= jnp.asarray(bucket_edges)).astype(jnp.int32), axis=-1)
    return jnp.where(distance < 16, distance, 16 + counted)


def mm(left, right):
    return jnp.dot(left, right, preferred_element_type=F32)


def mm_nt(left, right):
    return lax.dot_general(left, right, (((1,), (1,)), ((), ())), preferred_element_type=F32)


def mm_tn(left, right):
    return lax.dot_general(left, right, (((0,), (0,)), ((), ())), preferred_element_type=F32)


def choose(flag, left, right):
    return lax.select(flag, left, right)


def segments(bounds, shape, axis):
    place = lax.broadcasted_iota(jnp.int32, shape, axis)
    segment = jnp.zeros(shape, jnp.int32)
    for bound in bounds:
        segment = segment + (place >= bound).astype(jnp.int32)
    return segment


def read_bounds(info, seq_count):
    bounds, total = [], 0
    for index in range(seq_count):
        total = total + info[4 + index]
        bounds.append(total)
    return bounds


def rms_parts(values, gain):
    scale = lax.rsqrt(jnp.mean(values * values, axis=-1, keepdims=True) + EPS)
    return scale, (values * scale * gain).astype(BF16)


def rms_back(values, gain, grad):
    scale = lax.rsqrt(jnp.mean(values * values, axis=-1, keepdims=True) + EPS)
    weighted = grad * gain
    inner = jnp.mean(weighted * values, axis=-1, keepdims=True)
    grad_values = scale * weighted - values * (scale * scale * scale * inner)
    grad_gain = jnp.sum(grad * values * scale, axis=0, keepdims=True)
    return grad_values, grad_gain


def head_masks(rows):
    lane = lax.broadcasted_iota(jnp.int32, (rows, PAIR), 1)
    left = (lane < PAIR // 2).astype(F32)
    return left.astype(BF16), (1.0 - left).astype(BF16)


def attend(queries, keys, values, allowed, bias_of, probs_ref, out_ref):
    q_left, q_right = head_masks(queries.shape[0])
    k_left, k_right = head_masks(keys.shape[0])
    rows = queries.shape[0]
    for pair in range(HEADS // 2):
        lanes = slice(pair * PAIR, (pair + 1) * PAIR)
        query, key, value = queries[:, lanes], keys[:, lanes], values[:, lanes]
        scores = mm_nt(jnp.concatenate([query * q_left, query * q_right], axis=0), key)
        probs = []
        for side in range(2):
            part = scores[side * rows : (side + 1) * rows]
            if bias_of is not None:
                part = part + bias_of(2 * pair + side)
            part = jnp.where(allowed, part, NEG)
            raised = jnp.exp(part - jnp.max(part, axis=-1, keepdims=True))
            weights = raised / jnp.sum(raised, axis=-1, keepdims=True)
            probs_ref[2 * pair + side] = weights
            probs.append(weights.astype(BF16))
        both = jnp.concatenate([value * k_left, value * k_right], axis=0)
        out_ref[:, lanes] = mm(jnp.concatenate(probs, axis=1), both).astype(BF16)


def attend_back(queries, keys, values, grad_out, probs_ref, dq_ref, dk_ref, dv_ref, collect):
    q_left, q_right = head_masks(queries.shape[0])
    k_left, k_right = head_masks(keys.shape[0])
    rows = queries.shape[0]
    for pair in range(HEADS // 2):
        lanes = slice(pair * PAIR, (pair + 1) * PAIR)
        query, key, value, grad = queries[:, lanes], keys[:, lanes], values[:, lanes], grad_out[:, lanes]
        grad_two = jnp.concatenate([grad * q_left, grad * q_right], axis=0)
        query_two = jnp.concatenate([query * q_left, query * q_right], axis=0)
        key_two = jnp.concatenate([key * k_left, key * k_right], axis=0)
        grad_probs = mm_nt(grad_two, value)
        probs, scores = [], []
        for side in range(2):
            weights = probs_ref[2 * pair + side]
            part = grad_probs[side * rows : (side + 1) * rows]
            inner = jnp.sum(weights * part, axis=-1, keepdims=True)
            score = (weights * (part - inner)).astype(BF16)
            if collect is not None:
                collect(2 * pair + side, score)
            probs.append(weights.astype(BF16))
            scores.append(score)
        dq_ref[:, lanes] = mm(jnp.concatenate(scores, axis=1), key_two).astype(BF16)
        dk_ref[:, lanes] = mm_tn(jnp.concatenate(scores, axis=0), query_two).astype(BF16)
        dv_ref[:, lanes] = mm_tn(jnp.concatenate(probs, axis=0), grad_two).astype(BF16)


def owners_of(info):
    core, side = info[0], info[3]
    return 2 * core + side, 2 * core + 1 - side, 2 * (1 - core) + side, 2 * (1 - core) + 1 - side


def load_weights(info, mine, theirs, weights, sems):
    rows = weights.shape[2]
    copies = []
    for source, base in ((mine, 2 * info[0]), (theirs, 2 * (1 - info[0]))):
        for index in range(2):
            copy = pltpu.make_async_copy(
                source.at[:, pl.ds(index * rows, rows), :],
                weights.at[base + index],
                sems.at[len(copies)],
            )
            copy.start()
            copies.append(copy)
    return copies


def weight_grads(info, lefts, grads, targets):
    for target, place in zip(targets, owners_of(info)):
        left = lefts[place] if hasattr(lefts, "at") else choose(place == 3, lefts[1], lefts[0])
        target[...] = mm_tn(left, grads[place]).astype(BF16).reshape(target.shape)


def whole(weights, index):
    return weights[index].reshape(-1, weights.shape[-1])


def collect_kernel(high, info, *refs):
    pieces, out, sems = refs[:-2], refs[-2], refs[-1]
    copies = []
    for step in range(high):
        owner = lax.bitwise_xor(info[1], step) * 2
        for other, place in ((0, owner + info[2]), (1, owner + 1 - info[2])):
            copy = pltpu.make_async_copy(
                pieces[2 * step + other], out.at[place], sems.at[2 * step + other]
            )
            copy.start()
            copies.append(copy)
    for copy in copies:
        copy.wait()


def self_forward(seq_count, info, tokens, gain, line, mine, theirs, q_out, k_out, v_out, probs, attn, hidden, weights, sems):
    copies = load_weights(info, mine, theirs, weights, sems)
    rows = tokens.shape[0]
    values = tokens[...].astype(F32)
    _, normed = rms_parts(values, gain[...])
    bounds = read_bounds(info, seq_count)
    allowed = segments(bounds, (rows, rows), 0) == segments(bounds, (rows, rows), 1)
    allowed = allowed & (
        lax.broadcasted_iota(jnp.int32, (rows, rows), 0) >= lax.broadcasted_iota(jnp.int32, (rows, rows), 1)
    )
    live = (segments(bounds, (rows, 1), 0) < seq_count).astype(F32)

    def bias_of(head):
        wide = jnp.broadcast_to(line[head : head + 1, :], (rows, rows))
        return pltpu.roll(wide, 0, 1, stride=1, stride_axis=0)

    for copy in copies:
        copy.wait()
    q_out[...] = mm(normed, whole(weights, 0)).astype(BF16)
    k_out[...] = mm(normed, whole(weights, 1)).astype(BF16)
    v_out[...] = mm(normed, whole(weights, 2)).astype(BF16)
    attend(q_out[...], k_out[...], v_out[...], allowed, bias_of, probs, attn)
    hidden[...] = values + live * mm(attn[...], whole(weights, 3))


def cross_forward(seq_count, info, hidden_one, gain, gain_next, encoder, mine, theirs, q_out, k_out, v_out, probs, attn, hidden, normed_out, weights, sems):
    copies = load_weights(info, mine, theirs, weights, sems)
    rows, enc_rows = hidden_one.shape[0], encoder.shape[0]
    values = hidden_one[...]
    _, normed = rms_parts(values, gain[...])
    bounds = read_bounds(info, seq_count)
    clipped = jnp.minimum(segments(bounds, (rows, enc_rows), 0), seq_count - 1)
    length = enc_rows // seq_count
    place = lax.broadcasted_iota(jnp.int32, (rows, enc_rows), 1)
    key_segment = jnp.zeros((rows, enc_rows), jnp.int32)
    for index in range(1, seq_count):
        key_segment = key_segment + (place >= index * length).astype(jnp.int32)
    allowed = clipped == key_segment
    live = (segments(bounds, (rows, 1), 0) < seq_count).astype(F32)
    for copy in copies:
        copy.wait()
    q_out[...] = mm(normed, whole(weights, 0)).astype(BF16)
    k_out[...] = mm(encoder[...], whole(weights, 1)).astype(BF16)
    v_out[...] = mm(encoder[...], whole(weights, 2)).astype(BF16)
    attend(q_out[...], k_out[...], v_out[...], allowed, None, probs, attn)
    result = values + live * mm(attn[...], whole(weights, 3))
    hidden[...] = result
    normed_out[...] = rms_parts(result, gain_next[...])[1]


def unpack_down(packed, owner, wide):
    sub = packed.shape[1] // 3
    return jnp.concatenate(
        [
            jnp.concatenate(
                [packed[owner, sub * g : sub * (g + 1), wide + PAIR * i : wide + PAIR * (i + 1)] for g in range(3)],
                axis=1,
            )
            for i in range(4)
        ],
        axis=0,
    )


def pack_down(target, owner, wide, values):
    sub = target.shape[1] // 3
    for i in range(4):
        for g in range(3):
            target[owner, sub * g : sub * (g + 1), wide + PAIR * i : wide + PAIR * (i + 1)] = values[
                sub * i : sub * (i + 1), PAIR * g : PAIR * (g + 1)
            ]


def feed_forward(last, seq_count, info, normed_ref, cotangent, mine, theirs, *refs):
    if last:
        hidden, gain, total, back, mixed, grad_hidden, grad_gain, g_mine, g_other = refs
    else:
        total_out, back_out, g_mine, g_other = refs
    flag = info[0] == 0
    rows, width = cotangent.shape
    half = width // 2
    count, _, packed = mine.shape
    wide = packed * 2 // 3
    units = wide // count
    owners = max(1, 256 // units)
    chunk = owners * units
    bounds = read_bounds(info, seq_count)
    live = (segments(bounds, (rows, 1), 0) < seq_count).astype(F32)
    normed = normed_ref[...]
    branch = (live * cotangent[...].astype(F32)).astype(BF16)
    left, right = branch[:, :half], branch[:, half:]
    b_mine, b_other = choose(flag, left, right), choose(flag, right, left)
    if last:
        sum_mine, sum_other, sum_back = total[0], total[1], back[...]
    else:
        sum_mine = jnp.zeros((rows, half), F32)
        sum_other = jnp.zeros((rows, half), F32)
        sum_back = jnp.zeros((rows, width), F32)
    for step in range(wide // chunk):
        lanes = slice(step * chunk, (step + 1) * chunk)
        places = range(step * owners, (step + 1) * owners)
        own = mine[:, :, lanes].reshape(width, chunk)
        other = theirs[:, :, lanes].reshape(width, chunk)
        down_own = jnp.concatenate([unpack_down(mine, o, wide) for o in places], axis=0)
        down_other = jnp.concatenate([unpack_down(theirs, o, wide) for o in places], axis=0)
        first, second = mm(normed, own), mm(normed, other)
        gate, up = choose(flag, first, second), choose(flag, second, first)
        inner = jnp.tanh(SQRT_2_PI * (gate + 0.044715 * (gate * gate * gate)))
        cdf = 0.5 * (1.0 + inner)
        gelu = gate * cdf
        act = (gelu * up).astype(BF16)
        sum_mine += mm(act, down_own)
        sum_other += mm(act, down_other)
        d_act = mm_nt(b_mine, down_own) + mm_nt(b_other, down_other)
        slope = cdf + 0.5 * gate * (1.0 - inner * inner) * (
            SQRT_2_PI * (1.0 + 3 * 0.044715 * (gate * gate))
        )
        d_gate = (d_act * up * slope).astype(BF16)
        d_up = (d_act * gelu).astype(BF16)
        d_own, d_other = choose(flag, d_gate, d_up), choose(flag, d_up, d_gate)
        sum_back += mm_nt(d_own, own) + mm_nt(d_other, other)
        g_mine[:, :, lanes] = mm_tn(normed, d_own).astype(BF16).reshape(count, -1, chunk)
        g_other[:, :, lanes] = mm_tn(normed, d_other).astype(BF16).reshape(count, -1, chunk)
        down_grad = mm_tn(act, b_mine).astype(BF16)
        down_grad_other = mm_tn(act, b_other).astype(BF16)
        for index, owner in enumerate(places):
            here = slice(index * units, (index + 1) * units)
            pack_down(g_mine, owner, wide, down_grad[here])
            pack_down(g_other, owner, wide, down_grad_other[here])
    if last:
        outcome = jnp.concatenate(
            [choose(flag, sum_mine, sum_other), choose(flag, sum_other, sum_mine)], axis=1
        )
        mixed[...] = (hidden[...] + live * outcome).astype(BF16)
        part, term = rms_back(hidden[...], gain[...], sum_back)
        grad_hidden[...] = cotangent[...].astype(F32) + part
        grad_gain[...] = term
    else:
        total_out[0] = sum_mine
        total_out[1] = sum_other
        back_out[...] = sum_back


def cross_backward(
    seq_count, info, grad_in, hidden_one, gain, encoder, queries, keys, values, probs, attn, mine, theirs,
    grad_out, grad_enc, grad_gain, g_own, g_side, g_core, g_far, weights, grads, lefts, sems,
):
    copies = load_weights(info, mine, theirs, weights, sems)
    rows = hidden_one.shape[0]
    bounds = read_bounds(info, seq_count)
    live = (segments(bounds, (rows, 1), 0) < seq_count).astype(F32)
    grad = grad_in[...]
    branch = (live * grad).astype(BF16)
    _, normed = rms_parts(hidden_one[...], gain[...])
    lefts[0] = normed
    lefts[1] = encoder[...]
    lefts[2] = encoder[...]
    lefts[3] = attn[...]
    grads[3] = branch
    for copy in copies:
        copy.wait()
    grad_attn = mm_nt(branch, whole(weights, 3)).astype(BF16)
    attend_back(queries[...], keys[...], values[...], grad_attn, probs, grads.at[0], grads.at[1], grads.at[2], None)
    weight_grads(info, lefts, grads, (g_own, g_side, g_core, g_far))
    d_query, d_key, d_value = grads[0], grads[1], grads[2]
    grad_enc[...] = mm_nt(d_key, whole(weights, 1)) + mm_nt(d_value, whole(weights, 2))
    part, term = rms_back(hidden_one[...], gain[...], mm_nt(d_query, whole(weights, 0)))
    grad_out[...] = grad + part
    grad_gain[...] = term


def self_backward(
    seq_count, info, grad_in, tokens, gain, queries, keys, values, probs, attn, mine, theirs,
    grad_out, grad_gain, grad_line, g_own, g_side, g_core, g_far, weights, grads, sems,
):
    copies = load_weights(info, mine, theirs, weights, sems)
    rows = tokens.shape[0]
    bounds = read_bounds(info, seq_count)
    live = (segments(bounds, (rows, 1), 0) < seq_count).astype(F32)
    grad = grad_in[...]
    branch = (live * grad).astype(BF16)
    inputs = tokens[...].astype(F32)
    _, normed = rms_parts(inputs, gain[...])
    grad_line[...] = jnp.zeros_like(grad_line)
    grads[3] = branch
    place = lax.broadcasted_iota(jnp.int32, (rows, rows), 0)
    flip = (place + lax.broadcasted_iota(jnp.int32, (rows, rows), 1) == rows - 1).astype(F32).astype(BF16)

    def collect(head, score):
        turned = pltpu.roll(mm(flip, score), 1, 1, stride=1, stride_axis=0)
        grad_line[head : head + 1, :] = jnp.sum(turned, axis=0, keepdims=True)

    for copy in copies:
        copy.wait()
    grad_attn = mm_nt(branch, whole(weights, 3)).astype(BF16)
    attend_back(
        queries[...], keys[...], values[...], grad_attn, probs, grads.at[0], grads.at[1], grads.at[2], collect
    )
    weight_grads(info, (normed, attn[...]), grads, (g_own, g_side, g_core, g_far))
    d_query, d_key, d_value = grads[0], grads[1], grads[2]
    grad_normed = (
        mm_nt(d_query, whole(weights, 0)) + mm_nt(d_key, whole(weights, 1)) + mm_nt(d_value, whole(weights, 2))
    )
    part, term = rms_back(inputs, gain[...], grad_normed)
    grad_out[...] = grad + part
    grad_gain[...] = term


class Links:
    def __init__(self, fsdp_count, replica_count):
        self.count = fsdp_count
        self.high = fsdp_count // 2
        self.replicas = replica_count
        self.place = lax.axis_index("fsdp")
        self.mine_high = self.place // 2
        self.mine_low = self.place % 2
        self.core = lax.axis_index("replica") % 2
        self.side = lax.axis_index("replica") // 2 % 2

    def swap_replica(self, values, bit):
        pairs = [(i, i ^ bit) for i in range(self.replicas)]
        return lax.ppermute(values, "replica", pairs)

    def swap_low(self, values):
        return lax.ppermute(values, "fsdp", [(i, i ^ 1) for i in range(self.count)])

    def swap_high(self, values, step):
        return lax.ppermute(values, "fsdp", [(i, i ^ (2 * step)) for i in range(self.count)])

    def collect(self, info, pieces):
        local = pieces[0]
        nbytes = 2 * len(pieces) * local.size * 2
        return pl.pallas_call(
            functools.partial(collect_kernel, self.high),
            out_shape=jax.ShapeDtypeStruct((self.count,) + local.shape, local.dtype),
            in_specs=[SMEM] + [ANY] * len(pieces),
            out_specs=ANY,
            scratch_shapes=[pltpu.SemaphoreType.DMA((len(pieces),))],
            compiler_params=params(16),
            cost_estimate=cost(0, nbytes),
        )(info, *pieces)

    def gather(self, locals_, window):
        got, sent, order = {}, [], []
        for index, local in enumerate(locals_):
            got[index, 0, 0] = local
            ring = []
            bit = self.high // 2
            keys = [0]
            while bit:
                for key in list(keys):
                    keys.append(key | bit)
                    ring.append(((index, key, 0), (index, key | bit, 0), bit))
                bit //= 2
            side = [((index, key, 0), (index, key, 1), 0) for key in keys]
            order.append((ring, side))
        queue, pending = [], []
        for ring, side in order:
            side = list(side)
            for item in ring:
                queue.append(item)
                if pending:
                    queue.append(pending.pop(0))
                elif side:
                    queue.append(side.pop(0))
            pending += side
        queue += pending
        ready = set((i, 0, 0) for i in range(len(locals_)))
        waiting = list(queue)
        queue = []
        while waiting:
            place = next(i for i, item in enumerate(waiting) if item[0] in ready)
            item = waiting.pop(place)
            ready.add(item[1])
            queue.append(item)
        for number, (source, target, bit) in enumerate(queue):
            values = got[source]
            if number >= window:
                old = queue[number - window][1]
                if old != source:
                    values, got[old] = lax.optimization_barrier((values, got[old]))
            got[target] = self.swap_high(values, bit) if bit else self.swap_low(values)
        return [
            [got[index, key, side] for key in range(self.high) for side in range(2)]
            for index in range(len(locals_))
        ]

    def split(self, values):
        values = values.reshape((self.high, 2) + values.shape[1:])
        return pick(values, 1 - self.mine_low, 1), pick(values, self.mine_low, 1)


class Sequence:
    def __init__(self, token):
        self.token = token

    def __call__(self, values):
        return after(values, self.token)[0]

    def mark(self, values):
        self.token = values
        return values


class Sums:
    def __init__(self, comm, sequence):
        self.comm, self.sequence = comm, sequence

    def low(self, *parts):
        parts = list(parts)
        parts[0] = self.sequence(parts[0])
        pairs = [self.comm.split(part) for part in parts]
        self.home = [pair[1] for pair in pairs]
        sent = self.sequence.mark(add(*[pair[0] for pair in pairs]))
        self.got = self.comm.swap_low(sent)
        self.bit = 0

    def step(self):
        comm = self.comm
        if not self.bit:
            total = add(self.sequence(self.got), *self.home)
            self.held = {key: pick(total, comm.mine_high ^ key, 0) for key in range(comm.high)}
            self.bit = 1
        else:
            self.receive()
            self.bit *= 2
        if self.bit >= comm.high:
            return False
        self.away = [key for key in self.held if key & self.bit]
        sent = self.sequence.mark(jnp.stack([self.held.pop(key) for key in self.away]))
        self.got = comm.swap_high(sent, self.bit)
        return True

    def receive(self):
        got = self.sequence(self.got)
        for index, key in enumerate(self.away):
            self.held[key ^ self.bit] = add(self.held[key ^ self.bit], got[index])

    def finish(self):
        while self.step():
            pass
        return self.sequence.mark(self.held[0])

    def over_replicas(self, values, bit):
        while bit < self.comm.replicas:
            values = add(values, self.comm.swap_replica(values, bit))
            bit *= 2
        return values


def add(*terms):
    return functools.reduce(jnp.add, [term.astype(F32) for term in terms]).astype(BF16)


def pick(values, index, axis):
    return lax.dynamic_index_in_dim(values, index, axis, keepdims=False)


def after(values, *tokens):
    return lax.optimization_barrier((values,) + tokens)


def per_device(
    sizes,
    tokens,
    encoded,
    lengths,
    cotangent,
    norm_self,
    q_self,
    k_self,
    v_self,
    o_self,
    bias_table,
    norm_cross,
    q_cross,
    k_cross,
    v_cross,
    o_cross,
    norm_ff,
    wi_gate,
    wi_up,
    wo_ff,
):
    count, replica_count = sizes
    comm = Links(count, replica_count)
    core_zero = comm.core == 0
    row_count, width = tokens.shape[1:]
    seq_count = lengths.shape[1]
    encoder = encoded[0].reshape(-1, width)
    enc_rows = encoder.shape[0]
    rows = q_self.shape[0]
    hidden_units = wi_gate.shape[1]
    down_rows = wo_ff.shape[0]
    half = width // 2
    info = jnp.concatenate(
        [jnp.stack([comm.core, comm.mine_high, comm.mine_low, comm.side]), lengths[0]]
    ).astype(jnp.int32)
    small = jnp.concatenate([norm_self, norm_cross, norm_ff, bias_table.reshape(-1)])
    small_count = small.shape[0]
    small = jnp.pad(small[None], ((0, 15), (0, width - small_count)))

    units = down_rows // 2
    side_zero = comm.side == 0
    wide = jnp.where(core_zero, wi_gate, wi_up).reshape(rows, count, 2, units)

    wide = pick(wide, comm.side, 2).reshape(rows, -1)
    down = pick(wo_ff.reshape(2, units, width), comm.side, 0)
    down = jnp.where(core_zero, down[:, :half], down[:, half:])
    down = down.reshape(4, units // 4, 3, PAIR).transpose(2, 1, 0, 3).reshape(rows, -1)
    feed_local = jnp.concatenate([wide, down], axis=1)
    first_local = jnp.concatenate(
        [jnp.where(core_zero, q_self, v_self), jnp.where(core_zero, k_self, o_self), small]
    )
    second_local = jnp.concatenate(
        [jnp.where(core_zero, q_cross, v_cross), jnp.where(core_zero, k_cross, o_cross)]
    )
    feed_pieces, first_pieces, second_pieces = comm.gather(
        [feed_local, first_local, second_local], 4
    )
    feed_one = comm.collect(info, feed_pieces)
    feed_two = comm.swap_replica(feed_one, 2)
    feed_one_theirs = comm.swap_replica(feed_one, 1)
    first_mine = comm.collect(info, first_pieces)
    first_theirs = comm.swap_replica(first_mine, 1)

    vectors = first_mine[:, 2 * rows, :small_count].astype(F32)
    gain_one = vectors[:, :rows].reshape(1, -1)
    gain_two = vectors[:, rows : 2 * rows].reshape(1, -1)
    gain_three = vectors[:, 2 * rows : 3 * rows].reshape(1, -1)
    table = vectors[:, 3 * rows :].reshape(-1, HEADS)
    turned = jnp.asarray((-np.arange(row_count)) % row_count, jnp.int32)
    bucket_hot = (
        bucket_of(turned)[:, None] == lax.iota(jnp.int32, table.shape[0])[None, :]
    ).astype(F32)
    line = jnp.dot(bucket_hot, table, precision=lax.Precision.HIGHEST).T
    line = jnp.pad(line, ((0, 16 - HEADS), (0, 0)))

    def shape(*dims, dtype=BF16):
        return jax.ShapeDtypeStruct(dims, dtype)

    act = shape(row_count, width)
    act_enc = shape(enc_rows, width)
    act32 = shape(row_count, width, dtype=F32)
    vec32 = shape(1, width, dtype=F32)
    weight_scratch = pltpu.VMEM((4, count, rows, width), BF16)
    sems = pltpu.SemaphoreType.DMA((4,))
    weight_bytes = 4 * count * rows * width * 2
    pair_flops = 2 * row_count * width * width
    attn_scratch = pltpu.VMEM((4, row_count, width), BF16)

    tokens_here = tokens[0]
    queries, keys, values, probs, attn_one, hidden_one = pl.pallas_call(
        functools.partial(self_forward, seq_count),
        out_shape=(act, act, act, shape(HEADS, row_count, row_count, dtype=F32), act, act32),
        in_specs=[SMEM, VMEM, VMEM, VMEM] + [ANY] * 2,
        out_specs=[VMEM] * 6,
        scratch_shapes=[weight_scratch, sems],
        compiler_params=params(),
        cost_estimate=cost(5 * pair_flops, weight_bytes),
    )(info, tokens_here, gain_one, line, first_mine, first_theirs)

    second_mine = comm.collect(info, second_pieces)
    second_theirs = comm.swap_replica(second_mine, 1)
    feed_two_theirs = comm.swap_replica(feed_two, 1)
    queries_c, keys_c, values_c, probs_c, attn_two, hidden_two, normed_three = pl.pallas_call(
        functools.partial(cross_forward, seq_count),
        out_shape=(act, act_enc, act_enc, shape(HEADS, row_count, enc_rows, dtype=F32), act, act32, act),
        in_specs=[SMEM, VMEM, VMEM, VMEM, VMEM] + [ANY] * 2,
        out_specs=[VMEM] * 7,
        scratch_shapes=[weight_scratch, sems],
        compiler_params=params(),
        cost_estimate=cost(5 * pair_flops, weight_bytes),
    )(info, hidden_one, gain_two, gain_three, encoder, second_mine, second_theirs)

    packed = shape(*feed_one.shape)
    feed_cost = cost(9 * row_count * width * hidden_units, 12 * width * hidden_units)
    total, back, g_one, g_one_other = pl.pallas_call(
        functools.partial(feed_forward, False, seq_count),
        out_shape=(shape(2, row_count, half, dtype=F32), act32, packed, packed),
        in_specs=[SMEM] + [VMEM] * 4,
        out_specs=[VMEM] * 4,
        compiler_params=params(),
        cost_estimate=feed_cost,
    )(info, normed_three, cotangent[0], feed_one, feed_one_theirs)
    mixed, grad_hidden_two, grad_norm_three, g_two, g_two_other = pl.pallas_call(
        functools.partial(feed_forward, True, seq_count),
        out_shape=(act, act32, vec32, packed, packed),
        in_specs=[SMEM] + [VMEM] * 8,
        out_specs=[VMEM] * 5,
        compiler_params=params(),
        cost_estimate=feed_cost,
    )(info, normed_three, cotangent[0], feed_two, feed_two_theirs, hidden_two, gain_three, total, back)

    sequence = Sequence(grad_norm_three)
    one, two, second, first = (Sums(comm, sequence) for _ in range(4))
    one_got = comm.swap_replica(g_one_other, 1)
    two_got = comm.swap_replica(g_two_other, 1)
    one.low(g_one, one_got)
    grad_hidden_two = sequence(grad_hidden_two)

    grads = shape(count, rows, width)
    grad_hidden_one, grad_encoder, grad_norm_two, *g_second = pl.pallas_call(
        functools.partial(cross_backward, seq_count),
        out_shape=(act32, shape(enc_rows, width, dtype=F32), vec32) + (grads,) * 4,
        in_specs=[SMEM] + [VMEM] * 9 + [ANY] * 2,
        out_specs=[VMEM] * 7,
        scratch_shapes=[weight_scratch, attn_scratch, attn_scratch, sems],
        compiler_params=params(),
        cost_estimate=cost(10 * pair_flops, 2 * weight_bytes),
    )(
        info, grad_hidden_two, hidden_one, gain_two, encoder, queries_c, keys_c, values_c, probs_c, attn_two,
        second_mine, second_theirs,
    )
    def across(g_own, g_side, g_core, g_far):
        from_far = comm.swap_replica(g_far, 1)
        from_core = comm.swap_replica(g_core, 1)

        def finish():
            side = sequence.mark(add(sequence(from_far), g_side))
            return g_own, from_core, comm.swap_replica(side, 2)

        return finish

    sequence.mark(grad_norm_two)
    two.low(g_two, two_got)
    second_parts = across(*g_second)()
    grad_hidden_one = sequence(grad_hidden_one)

    grad_inputs, grad_norm_one, grad_line, *g_first = pl.pallas_call(
        functools.partial(self_backward, seq_count),
        out_shape=(act32, vec32, shape(16, row_count, dtype=F32)) + (grads,) * 4,
        in_specs=[SMEM] + [VMEM] * 8 + [ANY] * 2,
        out_specs=[VMEM] * 7,
        scratch_shapes=[weight_scratch, attn_scratch, sems],
        compiler_params=params(),
        cost_estimate=cost(10 * pair_flops, 2 * weight_bytes),
    )(
        info, grad_hidden_one, tokens_here, gain_one, queries, keys, values, probs, attn_one,
        first_mine, first_theirs,
    )
    sequence.mark(grad_norm_one)
    first_across = across(*g_first)
    one.step()
    second.low(*second_parts)
    first_parts = first_across()
    grad_table = jnp.dot(grad_line[:HEADS], bucket_hot, precision=lax.Precision.HIGHEST).T
    table_row = jnp.pad(grad_table.reshape(1, -1), ((0, 0), (0, width - grad_table.size)))
    vectors = jnp.concatenate([grad_norm_one, grad_norm_two, grad_norm_three, table_row])
    steps = [("replica", 1 << k) for k in range(replica_count.bit_length() - 1)]
    steps += [("fsdp", 1 << k) for k in range(count.bit_length() - 1)]

    def small_step():
        axis, bit = steps.pop(0)
        size = replica_count if axis == "replica" else count
        return lax.ppermute(sequence(vectors), axis, [(i, i ^ bit) for i in range(size)])

    def small_sum(got):
        return vectors + sequence(got)

    got = small_step()
    one.step()
    two.step()
    vectors = small_sum(got)
    got = small_step()
    second.step()
    first.low(*first_parts)
    vectors = small_sum(got)
    got = small_step()
    one_part = one.finish()
    two.step()
    second.step()
    vectors = small_sum(got)
    got = small_step()
    first.step()
    vectors = small_sum(got)
    got = small_step()
    two_part = two.finish()
    one_cross, two_cross = comm.swap_replica(two_part, 2), comm.swap_replica(one_part, 2)
    first.step()
    second_sum = second.over_replicas(second.finish(), 4)
    second_cross, second_core = comm.swap_replica(second_sum, 2), comm.swap_replica(second_sum, 1)
    one_sum = one.over_replicas(add(one_part, sequence(one_cross)), 4)
    two_sum = two.over_replicas(add(two_part, two_cross), 4)
    sequence.mark(two_sum)
    there = comm.swap_replica(one_sum, 1), comm.swap_replica(two_sum, 1)
    vectors = small_sum(got)
    while steps:
        vectors = small_sum(small_step())
    first_sum = first.over_replicas(first.finish(), 4)
    first_cross, first_core = comm.swap_replica(first_sum, 2), comm.swap_replica(first_sum, 1)
    second_far = comm.swap_replica(second_cross, 1)
    first_far = comm.swap_replica(first_cross, 1)

    def four(own, across, core, far):
        zero, one = jnp.where(side_zero, own, across), jnp.where(side_zero, across, own)
        two, three = jnp.where(side_zero, core, far), jnp.where(side_zero, far, core)
        return [
            jnp.where(core_zero, left, right).astype(F32)
            for left, right in ((zero, two), (one, three), (two, zero), (three, one))
        ]

    owned = lax.dynamic_slice(vectors, (0, comm.place * rows), (3, rows))
    table_size = bias_table.size
    owned_table = lax.dynamic_slice(vectors[3], (comm.place * table_size,), (table_size,))

    second = four(second_sum, second_cross, second_core, second_far)
    def by_side(one, two):
        return jnp.where(side_zero, one, two), jnp.where(side_zero, two, one)

    here, there = by_side(one_sum, two_sum), by_side(*there)
    wide_units = hidden_units // 2

    def wide_grad(parts):
        parts = [part[:, :wide_units].reshape(rows, count, 1, units) for part in parts]
        return jnp.concatenate(parts, axis=2).reshape(rows, hidden_units).astype(F32)

    def down_grad(parts):
        parts = [
            part[:, wide_units:].reshape(3, units // 4, 4, PAIR).transpose(2, 1, 0, 3).reshape(units, half)
            for part in parts
        ]
        return jnp.concatenate(parts, axis=0)

    low = [jnp.where(core_zero, one, two) for one, two in zip(here, there)]
    high = [jnp.where(core_zero, two, one) for one, two in zip(here, there)]
    grad_down = jnp.concatenate([down_grad(low), down_grad(high)], axis=1).astype(F32)
    grad_gate, grad_up = wide_grad(low), wide_grad(high)
    first = four(first_sum, first_cross, after(first_core, grad_gate, grad_up, grad_down, *second)[0], first_far)
    return (
        mixed[None],
        grad_inputs[None],
        grad_encoder.reshape(encoded.shape),
        owned[0],
        first[0],
        first[1],
        first[2],
        first[3],
        owned_table.reshape(bias_table.shape),
        owned[1],
        second[0],
        second[1],
        second[2],
        second[3],
        owned[2],
        grad_gate,
        grad_up,
        grad_down,
    )


def solution(mesh):
    slots = P(("replica", "fsdp"), None, None)
    slots_four = P(("replica", "fsdp"), None, None, None)
    vector, matrix = P("fsdp"), P("fsdp", None)
    weights = (
        (vector,) + (matrix,) * 5 + (vector,) + (matrix,) * 4 + (vector,) + (matrix,) * 3
    )
    return jax.shard_map(
        functools.partial(per_device, (mesh.shape["fsdp"], mesh.shape["replica"])),
        mesh=mesh,
        in_specs=(slots, slots_four, P(("replica", "fsdp"), None), slots) + weights,
        out_specs=(slots, slots, slots_four) + weights,
        check_vma=False,
    )
```

profile of v0, /device:TPU:0, one launch (start us, length us, event | category | flops | bytes accessed | tf_op | source)
XLA Modules:
  0.0 282.4 jit_solution(1028932573714526133)
XLA Ops:
  3.6 4.1 %collective-permute-start = (bf16[96,1536]{1,0:T(8,128)(2,1)S(1)}, bf16[96,1536]{1,0:T(8,128)(2,1)S(1)}, u32[]{:S(2)}, u32[]{:S(2)}) collective-permute-start(bf16[96,1536]{1,0:T(8,128)(2,1)S(1)} %bitcast_dynamic-update-slice_fusion.1.refs_0_), channel_id=1, source_target_pairs={{0,4},{1,5},{2,6},{3,7},{4,0},{5,1},{6,2},{7,3},{8,12},{9,13},{10,... | collective-permute-start | bytes 884744 | tf_op jit(solution)/shard_map/ppermute | solution.py:412
  10.8 10.3 %collective-permute-done.refs_4_ = bf16[96,1536]{1,0:T(8,128)(2,1)S(1)} collective-permute-done((bf16[96,1536]{1,0:T(8,128)(2,1)S(1)}, bf16[96,1536]{1,0:T(8,128)(2,1)S(1)}, u32[]{:S(2)}, u32[]{:S(2)}) %collective-permute-start) | collective-permute-done | bytes 294944 | tf_op jit(solution)/shard_map/ppermute | solution.py:412
  24.2 3.4 %collective-permute-start.8 = (bf16[208,768]{1,0:T(8,128)(2,1)S(1)}, bf16[208,768]{1,0:T(8,128)(2,1)S(1)}, u32[]{:S(2)}, u32[]{:S(2)}) collective-permute-start(bf16[208,768]{1,0:T(8,128)(2,1)S(1)} %fusion.9.refs_0_), channel_id=1, source_target_pairs={{0,4},{1,5},{2,6},{3,7},{4,0},{5,1},{6,2},{7,3},{8,12},{9,13},{10,... | collective-permute-start | bytes 958472 | tf_op jit(solution)/shard_map/ppermute | solution.py:412
  27.6 5.9 %collective-permute-done.1.refs_6_ = bf16[96,1536]{1,0:T(8,128)(2,1)S(1)} collective-permute-done((bf16[96,1536]{1,0:T(8,128)(2,1)S(1)}, bf16[96,1536]{1,0:T(8,128)(2,1)S(1)}, u32[]{:S(2)}, u32[]{:S(2)}) %collective-permute-start.1) | collective-permute-done | bytes 294944 | tf_op jit(solution)/shard_map/ppermute | solution.py:412
  53.5 4.9 %collective-permute-done.9.refs_6_ = bf16[208,768]{1,0:T(8,128)(2,1)S(1)} collective-permute-done((bf16[208,768]{1,0:T(8,128)(2,1)S(1)}, bf16[208,768]{1,0:T(8,128)(2,1)S(1)}, u32[]{:S(2)}, u32[]{:S(2)}) %collective-permute-start.9) | collective-permute-done | bytes 319520 | tf_op jit(solution)/shard_map/ppermute | solution.py:412
  66.4 3.9 %collective-permute-done.14.refs_2_ = bf16[192,768]{1,0:T(8,128)(2,1)S(1)} collective-permute-done((bf16[192,768]{1,0:T(8,128)(2,1)S(1)}, bf16[192,768]{1,0:T(8,128)(2,1)S(1)}, u32[]{:S(2)}, u32[]{:S(2)}) %collective-permute-start.14) | collective-permute-done | bytes 294944 | tf_op jit(solution)/shard_map/ppermute | solution.py:412
  71.1 5.1 %collective-permute-done.20.refs_6_ = bf16[192,768]{1,0:T(8,128)(2,1)S(1)} collective-permute-done((bf16[192,768]{1,0:T(8,128)(2,1)S(1)}, bf16[192,768]{1,0:T(8,128)(2,1)S(1)}, u32[]{:S(2)}, u32[]{:S(2)}) %collective-permute-start.20) | collective-permute-done | bytes 294944 | tf_op jit(solution)/shard_map/ppermute | solution.py:412
  79.9 4.5 %collective-permute-done.19.refs_5_ = bf16[192,768]{1,0:T(8,128)(2,1)S(1)} collective-permute-done((bf16[192,768]{1,0:T(8,128)(2,1)S(1)}, bf16[192,768]{1,0:T(8,128)(2,1)S(1)}, u32[]{:S(2)}, u32[]{:S(2)}) %collective-permute-start.19) | collective-permute-done | bytes 294944 | tf_op jit(solution)/shard_map/ppermute | solution.py:409
  84.4 6.3 %collective-permute-done.21.refs_7_ = bf16[192,768]{1,0:T(8,128)(2,1)S(1)} collective-permute-done((bf16[192,768]{1,0:T(8,128)(2,1)S(1)}, bf16[192,768]{1,0:T(8,128)(2,1)S(1)}, u32[]{:S(2)}, u32[]{:S(2)}) %collective-permute-start.21) | collective-permute-done | bytes 294944 | tf_op jit(solution)/shard_map/ppermute | solution.py:409
  90.7 5.1 %collective-permute-done.18.refs_3_ = bf16[192,768]{1,0:T(8,128)(2,1)S(1)} collective-permute-done((bf16[192,768]{1,0:T(8,128)(2,1)S(1)}, bf16[192,768]{1,0:T(8,128)(2,1)S(1)}, u32[]{:S(2)}, u32[]{:S(2)}) %collective-permute-start.18) | collective-permute-done | bytes 294944 | tf_op jit(solution)/shard_map/ppermute | solution.py:409
  102.1 6.1 %shard_map.341 = (bf16[128,768]{1,0:T(8,128)(2,1)}, bf16[128,768]{1,0:T(8,128)(2,1)}, bf16[128,768]{1,0:T(8,128)(2,1)}, f32[12,128,128]{2,1,0:T(8,128)}, bf16[128,768]{1,0:T(8,128)(2,1)}, /*index=5*/f32[128,768]{1,0:T(8,128)}) custom-call(s32[6]{0:T(128)} %copy-done.3, bf16[128,768]{1,0:T(8,128)(2,1)} %bitcast.168, f32[1,768]{1,0:T(1,128)} %reshape.231.gain, ...), custom_call_target="tpu_custom_call" | custom-call | flops 754974720 | bytes 4718592 | tf_op jit(solution)/shard_map/pallas_call | solution.py:637
  108.2 6.0 %shard_map.343 = (bf16[128,768]{1,0:T(8,128)(2,1)}, bf16[128,768]{1,0:T(8,128)(2,1)}, bf16[128,768]{1,0:T(8,128)(2,1)}, f32[12,128,128]{2,1,0:T(8,128)}, bf16[12...) custom-call(s32[6]{0:T(128)} %copy-done.3, f32[128,768]{1,0:T(8,128)} %get-tuple-element.129.hidden_one, ...), custom_call_target="tpu_custom_call" | custom-call | flops 754974720 | bytes 4718592 | tf_op jit(solution)/shard_map/pallas_call | solution.py:650
  114.2 9.6 %shard_map.345 = (f32[2,128,384]{2,1,0:T(8,128)}, f32[128,768]{1,0:T(8,128)}, bf16[8,96,1536]{2,1,0:T(8,128)(2,1)}, bf16[8,96,1536]{2,1,0:T(8,128)(2,1)}) custom-call(s32[6]{0:T(128)} %copy-done.3, bf16[128,768]{1,0:T(8,128)(2,1)} %get-tuple-element.133.normed_ref, bf16[128,768]{1,0:T(8,128)(2,1)} %bitcast.190, bf16[8,96,1536]{2,1,0:T(8,128)(2,1)} %shard_map.344.mine, ...), custom_call_target="tpu_custom_call" | custom-call | flops 1811939328 | bytes 18874368 | tf_op jit(solution)/shard_map/pallas_call | solution.py:662
  124.4 10.2 %shard_map.346 = (bf16[128,768]{1,0:T(8,128)(2,1)}, f32[128,768]{1,0:T(8,128)}, f32[1,768]{1,0:T(1,128)}, bf16[8,96,1536]{2,1,0:T(8,128)(2,1)}, bf16[8,96,1536]{2,1,0:T(8,128)(2,1)}) custom-call(s32[6]{0:T(128)} %copy-done.3, bf16[128,768]{1,0:T(8,128)(2,1)} %get-tuple-element.133.normed_ref, bf16[128,768]{1,0:T(8,128)(2,1)} %bitcast.191, ...), custom_call_target="tpu_custom_call" | custom-call | flops 1811939328 | bytes 18874368 | tf_op jit(solution)/shard_map/pallas_call | solution.py:670
  137.4 9.9 %shard_map.347 = (f32[128,768]{1,0:T(8,128)}, f32[128,768]{1,0:T(8,128)}, f32[1,768]{1,0:T(1,128)}, bf16[8,96,768]{2,1,0:T(8,128)(2,1)}, bf16[8,96,768]{2,1,0:T(...) custom-call(s32[6]{0:T(128)} %copy-done.3, f32[128,768]{1,0:T(8,128)} %get-tuple-element.149.grad_in, ...), custom_call_target="tpu_custom_call" | custom-call | flops 1509949440 | bytes 9437184 | tf_op jit(solution)/shard_map/pallas_call | solution.py:687
  155.5 10.5 %shard_map.348 = (f32[128,768]{1,0:T(8,128)}, f32[1,768]{1,0:T(1,128)}, f32[16,128]{1,0:T(8,128)}, bf16[8,96,768]{2,1,0:T(8,128)(2,1)}, bf16[8,96,768]{2,1,0:T(8...) custom-call(s32[6]{0:T(128)} %copy-done.3, f32[128,768]{1,0:T(8,128)} %get-tuple-element.163.grad_in, ...), custom_call_target="tpu_custom_call" | custom-call | flops 1509949440 | bytes 9437184 | tf_op jit(solution)/shard_map/pallas_call | solution.py:714
  165.9 11.1 %collective-permute-done.30 = bf16[4,96,1536]{2,1,0:T(8,128)(2,1)} collective-permute-done((bf16[4,96,1536]{2,1,0:T(8,128)(2,1)}, bf16[4,96,1536]{2,1,0:T(8,128)(2,1)}, u32[]{:S(2)}, u32[]{:S(2)}) %collective-permute-start.30) | collective-permute-done | bytes 1179680 | tf_op jit(solution)/shard_map/ppermute | solution.py:409
  188.5 7.7 %collective-permute-done.35 = bf16[2,96,1536]{2,1,0:T(8,128)(2,1)} collective-permute-done((bf16[2,96,1536]{2,1,0:T(8,128)(2,1)}, bf16[2,96,1536]{2,1,0:T(8,128)(2,1)}, u32[]{:S(2)}, u32[]{:S(2)}) %collective-permute-start.35) | collective-permute-done | bytes 589856 | tf_op jit(solution)/shard_map/ppermute | solution.py:412
  205.8 8.2 %collective-permute-done.37 = bf16[4,96,768]{2,1,0:T(8,128)(2,1)S(1)} collective-permute-done((bf16[4,96,768]{2,1,0:T(8,128)(2,1)S(1)}, bf16[4,96,768]{2,1,0:T(8,128)(2,1)S(1)}, u32[]{:S(2)}, u32[]{:S(2)}) %collective-permute-start.37) | collective-permute-done | bytes 589856 | tf_op jit(solution)/shard_map/ppermute | solution.py:409
  221.6 5.0 %collective-permute-done.42 = bf16[2,96,1536]{2,1,0:T(8,128)(2,1)S(1)} collective-permute-done((bf16[2,96,1536]{2,1,0:T(8,128)(2,1)S(1)}, bf16[2,96,1536]{2,1,0:T(8,128)(2,1)S(1)}, u32[]{:S(2)}, u32[]{:S(2)}) %collective-permute-start.42) | collective-permute-done | bytes 589856 | tf_op jit(solution)/shard_map/ppermute | solution.py:412
  227.4 5.5 %collective-permute-done.41 = bf16[2,96,768]{2,1,0:T(8,128)(2,1)S(1)} collective-permute-done((bf16[2,96,768]{2,1,0:T(8,128)(2,1)S(1)}, bf16[2,96,768]{2,1,0:T(8,128)(2,1)S(1)}, u32[]{:S(2)}, u32[]{:S(2)}) %collective-permute-start.41) | collective-permute-done | bytes 294944 | tf_op jit(solution)/shard_map/ppermute | solution.py:412
  239.2 7.0 %collective-permute-done.47 = bf16[1,96,1536]{2,1,0:T(8,128)(2,1)S(1)} collective-permute-done((bf16[1,96,1536]{2,1,0:T(8,128)(2,1)S(1)}, bf16[1,96,1536]{2,1,0:T(8,128)(2,1)S(1)}, u32[]{:S(2)}, u32[]{:S(2)}) %collective-permute-start.47) | collective-permute-done | bytes 294944 | tf_op jit(solution)/shard_map/ppermute | solution.py:412
  259.1 4.6 %collective-permute-done.50 = bf16[1,96,768]{2,1,0:T(8,128)(2,1)S(1)} collective-permute-done((bf16[1,96,768]{2,1,0:T(8,128)(2,1)S(1)}, bf16[1,96,768]{2,1,0:T(8,128)(2,1)S(1)}, u32[]{:S(2)}, u32[]{:S(2)}) %collective-permute-start.50) | collective-permute-done | bytes 147488 | tf_op jit(solution)/shard_map/ppermute | solution.py:412
  267.0 4.0 %collective-permute-done.51 = bf16[96,768]{1,0:T(8,128)(2,1)} collective-permute-done((bf16[96,768]{1,0:T(8,128)(2,1)}, bf16[96,768]{1,0:T(8,128)(2,1)}, u32[]{:S(2)}, u32[]{:S(2)}) %collective-permute-start.51) | collective-permute-done | bytes 147488 | tf_op jit(solution)/shard_map/ppermute | solution.py:406
  (266 shorter events, 121.5 us)
Async XLA Ops:
  3.6 17.5 %collective-permute-start = (bf16[96,1536]{1,0:T(8,128)(2,1)S(1)}, bf16[96,1536]{1,0:T(8,128)(2,1)S(1)}, u32[]{:S(2)}, u32[]{:S(2)}) collective-permute-start(bf16[96,1536]{1,0:T(8,128)(2,1)S(1)} %bitcast_dynamic-update-slice_fusion.1.refs_0_), channel_id=1, source_target_pairs={{0,4},{1,5},{2,6},{3,7},{4,0},{5,1},{6,2},{7,3},{8,12},{9,13},{10,... | collective-permute-start | bytes 884744 | tf_op jit(solution)/shard_map/ppermute | solution.py:412
  24.2 17.8 %collective-permute-start.8 = (bf16[208,768]{1,0:T(8,128)(2,1)S(1)}, bf16[208,768]{1,0:T(8,128)(2,1)S(1)}, u32[]{:S(2)}, u32[]{:S(2)}) collective-permute-start(bf16[208,768]{1,0:T(8,128)(2,1)S(1)} %fusion.9.refs_0_), channel_id=1, source_target_pairs={{0,4},{1,5},{2,6},{3,7},{4,0},{5,1},{6,2},{7,3},{8,12},{9,13},{10,... | collective-permute-start | bytes 958472 | tf_op jit(solution)/shard_map/ppermute | solution.py:412
  42.0 16.4 %collective-permute-start.9 = (bf16[208,768]{1,0:T(8,128)(2,1)S(1)}, bf16[208,768]{1,0:T(8,128)(2,1)S(1)}, u32[]{:S(2)}, u32[]{:S(2)}) collective-permute-start(bf16[208,768]{1,0:T(8,128)(2,1)S(1)} %collective-permute-done.8.refs_4_), channel_id=1, source_target_pairs={{0,2},{1,3},{2,0},{3,1},{4,6},{5,7},{6,4},{7,5},{8,10},{9,11},{10,... | collective-permute-start | bytes 958472 | tf_op jit(solution)/shard_map/ppermute | solution.py:412
  48.0 50.8 %collective-permute-start.23 = (bf16[8,96,1536]{2,1,0:T(8,128)(2,1)}, bf16[8,96,1536]{2,1,0:T(8,128)(2,1)}, u32[]{:S(2)}, u32[]{:S(2)}) collective-permute-start(bf16[8,96,1536]{2,1,0:T(8,128)(2,1)} %shard_map.344.mine), channel_id=1, source_target_pairs={{0,16},{8,24},{16,0},{24,8},{1,17},{9,25},{17,1},{25,9},{2,18},{10... | collective-permute-start | bytes 7077896 | tf_op jit(solution)/shard_map/ppermute | solution.py:406
  58.5 18.6 %collective-permute-start.15 = (bf16[208,768]{1,0:T(8,128)(2,1)S(1)}, bf16[208,768]{1,0:T(8,128)(2,1)S(1)}, u32[]{:S(2)}, u32[]{:S(2)}) collective-permute-start(bf16[208,768]{1,0:T(8,128)(2,1)S(1)} %collective-permute-done.9.refs_6_), channel_id=1, source_target_pairs={{0,1},{1,0},{2,3},{3,2},{4,5},{5,4},{6,7},{7,6},{8,9},{9,8},{10,11... | collective-permute-start | bytes 958472 | tf_op jit(solution)/shard_map/ppermute | solution.py:409
  77.0 18.7 %collective-permute-start.18 = (bf16[192,768]{1,0:T(8,128)(2,1)S(1)}, bf16[192,768]{1,0:T(8,128)(2,1)S(1)}, u32[]{:S(2)}, u32[]{:S(2)}) collective-permute-start(bf16[192,768]{1,0:T(8,128)(2,1)S(1)} %collective-permute-done.14.refs_2_), channel_id=1, source_target_pairs={{0,1},{1,0},{2,3},{3,2},{4,5},{5,4},{6,7},{7,6},{8,9},{9,8},{10,11... | collective-permute-start | bytes 884744 | tf_op jit(solution)/shard_map/ppermute | solution.py:409
  79.8 22.2 %collective-permute-start.16 = (bf16[8,208,768]{2,1,0:T(8,128)(2,1)S(1)}, bf16[8,208,768]{2,1,0:T(8,128)(2,1)}, u32[]{:S(2)}, u32[]{:S(2)}) collective-permute-start(bf16[8,208,768]{2,1,0:T(8,128)(2,1)S(1)} %shard_map.340.mine), channel_id=1, source_target_pairs={{0,8},{8,0},{16,24},{24,16},{1,9},{9,1},{17,25},{25,17},{2,10},{10... | collective-permute-start | bytes 7667720 | tf_op jit(solution)/shard_map/ppermute | solution.py:406
  97.9 16.3 %collective-permute-start.25 = (bf16[8,96,1536]{2,1,0:T(8,128)(2,1)}, bf16[8,96,1536]{2,1,0:T(8,128)(2,1)}, u32[]{:S(2)}, u32[]{:S(2)}) collective-permute-start(bf16[8,96,1536]{2,1,0:T(8,128)(2,1)} %shard_map.344.mine), channel_id=1, source_target_pairs={{0,8},{8,0},{16,24},{24,16},{1,9},{9,1},{17,25},{25,17},{2,10},{10... | collective-permute-start | bytes 7077896 | tf_op jit(solution)/shard_map/ppermute | solution.py:406
  98.9 25.5 %collective-permute-start.24 = (bf16[8,96,1536]{2,1,0:T(8,128)(2,1)}, bf16[8,96,1536]{2,1,0:T(8,128)(2,1)}, u32[]{:S(2)}, u32[]{:S(2)}) collective-permute-start(bf16[8,96,1536]{2,1,0:T(8,128)(2,1)} %collective-permute-done.23.mine), channel_id=1, source_target_pairs={{0,8},{8,0},{16,24},{24,16},{1,9},{9,1},{17,25},{25,17},{2,10},{10... | collective-permute-start | bytes 7077896 | tf_op jit(solution)/shard_map/ppermute | solution.py:406
  147.9 29.1 %collective-permute-start.30 = (bf16[4,96,1536]{2,1,0:T(8,128)(2,1)}, bf16[4,96,1536]{2,1,0:T(8,128)(2,1)}, u32[]{:S(2)}, u32[]{:S(2)}) collective-permute-start(bf16[4,96,1536]{2,1,0:T(8,128)(2,1)} %fusion.2), channel_id=1, source_target_pairs={{0,1},{1,0},{2,3},{3,2},{4,5},{5,4},{6,7},{7,6},{8,9},{9,8},{10,11... | collective-permute-start | bytes 3538952 | tf_op jit(solution)/shard_map/ppermute | solution.py:409
  148.9 33.0 %collective-permute-start.31 = (bf16[8,96,768]{2,1,0:T(8,128)(2,1)}, bf16[8,96,768]{2,1,0:T(8,128)(2,1)}, u32[]{:S(2)}, u32[]{:S(2)}) collective-permute-start(bf16[8,96,768]{2,1,0:T(8,128)(2,1)} %get-tuple-element.177), channel_id=1, source_target_pairs={{0,8},{8,0},{16,24},{24,16},{1,9},{9,1},{17,25},{25,17},{2,10},{10... | collective-permute-start | bytes 3538952 | tf_op jit(solution)/shard_map/ppermute | solution.py:406
  151.6 50.7 %collective-permute-start.34 = (bf16[4,96,1536]{2,1,0:T(8,128)(2,1)}, bf16[4,96,1536]{2,1,0:T(8,128)(2,1)}, u32[]{:S(2)}, u32[]{:S(2)}) collective-permute-start(bf16[4,96,1536]{2,1,0:T(8,128)(2,1)} %fusion.3), channel_id=1, source_target_pairs={{0,1},{1,0},{2,3},{3,2},{4,5},{5,4},{6,7},{7,6},{8,9},{9,8},{10,11... | collective-permute-start | bytes 3538952 | tf_op jit(solution)/shard_map/ppermute | solution.py:409
  154.0 28.5 %collective-permute-start.32 = (bf16[8,96,768]{2,1,0:T(8,128)(2,1)}, bf16[8,96,768]{2,1,0:T(8,128)(2,1)}, u32[]{:S(2)}, u32[]{:S(2)}) collective-permute-start(bf16[8,96,768]{2,1,0:T(8,128)(2,1)} %add_convert_fusion.1), channel_id=1, source_target_pairs={{0,16},{8,24},{16,0},{24,8},{1,17},{9,25},{17,1},{25,9},{2,18},{10... | collective-permute-start | bytes 3538952 | tf_op jit(solution)/shard_map/ppermute | solution.py:406
  182.0 35.2 %collective-permute-start.38 = (bf16[8,96,768]{2,1,0:T(8,128)(2,1)}, bf16[8,96,768]{2,1,0:T(8,128)(2,1)S(1)}, u32[]{:S(2)}, u32[]{:S(2)}) collective-permute-start(bf16[8,96,768]{2,1,0:T(8,128)(2,1)} %get-tuple-element.188), channel_id=1, source_target_pairs={{0,8},{8,0},{16,24},{24,16},{1,9},{9,1},{17,25},{25,17},{2,10},{10... | collective-permute-start | bytes 3538952 | tf_op jit(solution)/shard_map/ppermute | solution.py:406
  184.2 29.8 %collective-permute-start.37 = (bf16[4,96,768]{2,1,0:T(8,128)(2,1)S(1)}, bf16[4,96,768]{2,1,0:T(8,128)(2,1)S(1)}, u32[]{:S(2)}, u32[]{:S(2)}) collective-permute-start(bf16[4,96,768]{2,1,0:T(8,128)(2,1)S(1)} %fusion.7), channel_id=1, source_target_pairs={{0,1},{1,0},{2,3},{3,2},{4,5},{5,4},{6,7},{7,6},{8,9},{9,8},{10,11... | collective-permute-start | bytes 1769480 | tf_op jit(solution)/shard_map/ppermute | solution.py:409
  186.9 30.3 %collective-permute-start.39 = (bf16[8,96,768]{2,1,0:T(8,128)(2,1)S(1)}, bf16[8,96,768]{2,1,0:T(8,128)(2,1)S(1)}, u32[]{:S(2)}, u32[]{:S(2)}) collective-permute-start(bf16[8,96,768]{2,1,0:T(8,128)(2,1)S(1)} %add_convert_fusion), channel_id=1, source_target_pairs={{0,16},{8,24},{16,0},{24,8},{1,17},{9,25},{17,1},{25,9},{2,18},{10... | collective-permute-start | bytes 3538952 | tf_op jit(solution)/shard_map/ppermute | solution.py:406
  197.2 22.7 %collective-permute-start.43 = (bf16[1,96,1536]{2,1,0:T(8,128)(2,1)S(1)}, bf16[1,96,1536]{2,1,0:T(8,128)(2,1)S(1)}, u32[]{:S(2)}, u32[]{:S(2)}) collective-permute-start(bf16[1,96,1536]{2,1,0:T(8,128)(2,1)S(1)} %add_convert_fusion.13), channel_id=1, source_target_pairs={{0,4},{1,5},{2,6},{3,7},{4,0},{5,1},{6,2},{7,3},{8,12},{9,13},{10,... | collective-permute-start | bytes 884744 | tf_op jit(solution)/shard_map/ppermute | solution.py:412
  205.7 20.8 %collective-permute-start.42 = (bf16[2,96,1536]{2,1,0:T(8,128)(2,1)S(1)}, bf16[2,96,1536]{2,1,0:T(8,128)(2,1)S(1)}, u32[]{:S(2)}, u32[]{:S(2)}) collective-permute-start(bf16[2,96,1536]{2,1,0:T(8,128)(2,1)S(1)} %pad_maximum_fusion.1), channel_id=1, source_target_pairs={{0,2},{1,3},{2,0},{3,1},{4,6},{5,7},{6,4},{7,5},{8,10},{9,11},{10,... | collective-permute-start | bytes 1769480 | tf_op jit(solution)/shard_map/ppermute | solution.py:412
  214.0 19.0 %collective-permute-start.36 = (f32[4,768]{1,0:T(4,128)S(1)}, f32[4,768]{1,0:T(4,128)S(1)}, u32[]{:S(2)}, u32[]{:S(2)}) collective-permute-start(f32[4,768]{1,0:T(4,128)S(1)} %fusion.22), channel_id=1, source_target_pairs={{0,16},{8,24},{16,0},{24,8},{1,17},{9,25},{17,1},{25,9},{2,18},{10... | collective-permute-start | bytes 36872 | tf_op jit(solution)/shard_map/ppermute | solution.py:740
  218.8 18.3 %collective-permute-start.45 = (bf16[4,96,768]{2,1,0:T(8,128)(2,1)S(1)}, bf16[4,96,768]{2,1,0:T(8,128)(2,1)S(1)}, u32[]{:S(2)}, u32[]{:S(2)}) collective-permute-start(bf16[4,96,768]{2,1,0:T(8,128)(2,1)S(1)} %fusion.8), channel_id=1, source_target_pairs={{0,1},{1,0},{2,3},{3,2},{4,5},{5,4},{6,7},{7,6},{8,9},{9,8},{10,11... | collective-permute-start | bytes 1769480 | tf_op jit(solution)/shard_map/ppermute | solution.py:409
  221.0 27.8 %collective-permute-start.48 = (bf16[96,1536]{1,0:T(8,128)(2,1)S(1)}, bf16[96,1536]{1,0:T(8,128)(2,1)S(1)}, u32[]{:S(2)}, u32[]{:S(2)}) collective-permute-start(bf16[96,1536]{1,0:T(8,128)(2,1)S(1)} %fusion.10), channel_id=1, source_target_pairs={{0,16},{8,24},{16,0},{24,8},{1,17},{9,25},{17,1},{25,9},{2,18},{10... | collective-permute-start | bytes 884744 | tf_op jit(solution)/shard_map/ppermute | solution.py:406
  226.6 19.6 %collective-permute-start.47 = (bf16[1,96,1536]{2,1,0:T(8,128)(2,1)S(1)}, bf16[1,96,1536]{2,1,0:T(8,128)(2,1)S(1)}, u32[]{:S(2)}, u32[]{:S(2)}) collective-permute-start(bf16[1,96,1536]{2,1,0:T(8,128)(2,1)S(1)} %add_convert_fusion.11), channel_id=1, source_target_pairs={{0,4},{1,5},{2,6},{3,7},{4,0},{5,1},{6,2},{7,3},{8,12},{9,13},{10,... | collective-permute-start | bytes 884744 | tf_op jit(solution)/shard_map/ppermute | solution.py:412
  234.1 21.1 %collective-permute-start.54 = (bf16[1,96,768]{2,1,0:T(8,128)(2,1)S(1)}, bf16[1,96,768]{2,1,0:T(8,128)(2,1)S(1)}, u32[]{:S(2)}, u32[]{:S(2)}) collective-permute-start(bf16[1,96,768]{2,1,0:T(8,128)(2,1)S(1)} %add_convert_fusion.19), channel_id=1, source_target_pairs={{0,4},{1,5},{2,6},{3,7},{4,0},{5,1},{6,2},{7,3},{8,12},{9,13},{10,... | collective-permute-start | bytes 442376 | tf_op jit(solution)/shard_map/ppermute | solution.py:412
  237.5 17.3 %collective-permute-start.49 = (bf16[2,96,768]{2,1,0:T(8,128)(2,1)S(1)}, bf16[2,96,768]{2,1,0:T(8,128)(2,1)S(1)}, u32[]{:S(2)}, u32[]{:S(2)}) collective-permute-start(bf16[2,96,768]{2,1,0:T(8,128)(2,1)S(1)} %pad_maximum_fusion.4), channel_id=1, source_target_pairs={{0,2},{1,3},{2,0},{3,1},{4,6},{5,7},{6,4},{7,5},{8,10},{9,11},{10,... | collective-permute-start | bytes 884744 | tf_op jit(solution)/shard_map/ppermute | solution.py:412
  (66 other events, 899.5 us)
where the time goes:
time: 286 us; the launch traced here: 282 us
  waiting for transfers between devices  120 us (42%)
  Pallas kernels  58 us (20%)
  starting transfers between devices  57.5 us (20%)
  other arithmetic  31.2 us (11%)
  local copies, waits for them, and re-layouts  12.5 us (4%)
    ppermute x17, waiting for transfers between devices, swap_high(): lax.ppermute(values, 'fsdp', [(i, i ^ 2 * step) for i in range(self.count)])  63.7 us
    ppermute x16, waiting for transfers between devices, swap_low(): return lax.ppermute(values, 'fsdp', [(i, i ^ 1) for i in range(self.count)])  42.9 us
    ppermute x17, starting transfers between devices, swap_high(): lax.ppermute(values, 'fsdp', [(i, i ^ 2 * step) for i in range(self.count)])  23 us
    convert_element_type x19, other arithmetic, add(): functools.reduce(jnp.add, [term.astype(F32) for term in terms]).astype(BF16)  20.6 us
    ppermute x16, starting transfers between devices, swap_low(): return lax.ppermute(values, 'fsdp', [(i, i ^ 1) for i in range(self.count)])  19 us
    ppermute x23, starting transfers between devices, swap_replica(): return lax.ppermute(values, 'replica', pairs)  12.5 us
    pallas_call x1, Pallas kernels, per_device(): pl.pallas_call(functools.partial(self_backward, seq_count), out_shape=(ac...  10.5 us
    pallas_call x1, Pallas kernels, per_device(): pl.pallas_call(functools.partial(feed_forward, True, seq_count), out_shap...  10.2 us
  transfers between devices with their start and end apart: 61, of which 27 were waited for; matrix products, arithmetic and copies ran while one was open for 14% of the time, Pallas kernels for 21%

commit v1 on v0

--- a/solution.py
+++ b/solution.py
@@ -142,29 +142,43 @@
     return 2 * core + side, 2 * core + 1 - side, 2 * (1 - core) + side, 2 * (1 - core) + 1 - side
 
 
-def load_weights(info, mine, theirs, weights, sems):
-    rows = weights.shape[2]
+class Weights:
+    def __init__(self, info, mine, theirs, weights, sems, order):
+        self.weights, self.sems, self.source, self.ready = weights, sems, mine, set()
+        rows = weights.shape[2]
+        for place in order:
+            for here, source in ((info[0] == place // 2, mine), (info[0] != place // 2, theirs)):
+
+                @pl.when(here)
+                def _(place=place, source=source):
+                    pltpu.make_async_copy(
+                        source.at[:, pl.ds(place % 2 * rows, rows), :], weights.at[place], sems.at[place]
+                    ).start()
+
+    def __call__(self, index):
+        if index not in self.ready:
+            self.ready.add(index)
+            rows = self.weights.shape[2]
+            pltpu.make_async_copy(
+                self.source.at[:, pl.ds(0, rows), :], self.weights.at[index], self.sems.at[index]
+            ).wait()
+        return self.weights[index].reshape(-1, self.weights.shape[-1])
+
+
+def weight_grads(info, lefts, grads, held, targets, sems):
     copies = []
-    for source, base in ((mine, 2 * info[0]), (theirs, 2 * (1 - info[0]))):
-        for index in range(2):
-            copy = pltpu.make_async_copy(
-                source.at[:, pl.ds(index * rows, rows), :],
-                weights.at[base + index],
-                sems.at[len(copies)],
-            )
-            copy.start()
-            copies.append(copy)
+    *targets, far_one, far_two = targets
+    half = far_one.shape[0]
+    for index, place in enumerate(owners_of(info)):
+        held[index] = mm(lefts(place), grads[place]).astype(BF16).reshape(held.shape[1:])
+        if index < 3:
+            going = [(held.at[index], targets[index])]
+        else:
+            going = [(held.at[3, pl.ds(0, half)], far_one), (held.at[3, pl.ds(half, half)], far_two)]
+        for source, target in going:
+            copies.append(pltpu.make_async_copy(source, target, sems.at[len(copies)]))
+            copies[-1].start()
     return copies
-
-
-def weight_grads(info, lefts, grads, targets):
-    for target, place in zip(targets, owners_of(info)):
-        left = lefts[place] if hasattr(lefts, "at") else choose(place == 3, lefts[1], lefts[0])
-        target[...] = mm_tn(left, grads[place]).astype(BF16).reshape(target.shape)
-
-
-def whole(weights, index):
-    return weights[index].reshape(-1, weights.shape[-1])
 
 
 def collect_kernel(high, info, *refs):
@@ -183,7 +197,7 @@
 
 
 def self_forward(seq_count, info, tokens, gain, line, mine, theirs, q_out, k_out, v_out, probs, attn, hidden, weights, sems):
-    copies = load_weights(info, mine, theirs, weights, sems)
+    matrix = Weights(info, mine, theirs, weights, sems, (0, 1, 2, 3))
     rows = tokens.shape[0]
     values = tokens[...].astype(F32)
     _, normed = rms_parts(values, gain[...])
@@ -198,17 +212,15 @@
         wide = jnp.broadcast_to(line[head : head + 1, :], (rows, rows))
         return pltpu.roll(wide, 0, 1, stride=1, stride_axis=0)
 
-    for copy in copies:
-        copy.wait()
-    q_out[...] = mm(normed, whole(weights, 0)).astype(BF16)
-    k_out[...] = mm(normed, whole(weights, 1)).astype(BF16)
-    v_out[...] = mm(normed, whole(weights, 2)).astype(BF16)
+    q_out[...] = mm(normed, matrix(0)).astype(BF16)
+    k_out[...] = mm(normed, matrix(1)).astype(BF16)
+    v_out[...] = mm(normed, matrix(2)).astype(BF16)
     attend(q_out[...], k_out[...], v_out[...], allowed, bias_of, probs, attn)
-    hidden[...] = values + live * mm(attn[...], whole(weights, 3))
+    hidden[...] = values + live * mm(attn[...], matrix(3))
 
 
 def cross_forward(seq_count, info, hidden_one, gain, gain_next, encoder, mine, theirs, q_out, k_out, v_out, probs, attn, hidden, normed_out, weights, sems):
-    copies = load_weights(info, mine, theirs, weights, sems)
+    matrix = Weights(info, mine, theirs, weights, sems, (0, 1, 2, 3))
     rows, enc_rows = hidden_one.shape[0], encoder.shape[0]
     values = hidden_one[...]
     _, normed = rms_parts(values, gain[...])
@@ -221,13 +233,11 @@
         key_segment = key_segment + (place >= index * length).astype(jnp.int32)
     allowed = clipped == key_segment
     live = (segments(bounds, (rows, 1), 0) < seq_count).astype(F32)
-    for copy in copies:
-        copy.wait()
-    q_out[...] = mm(normed, whole(weights, 0)).astype(BF16)
-    k_out[...] = mm(encoder[...], whole(weights, 1)).astype(BF16)
-    v_out[...] = mm(encoder[...], whole(weights, 2)).astype(BF16)
+    q_out[...] = mm(normed, matrix(0)).astype(BF16)
+    k_out[...] = mm(encoder[...], matrix(1)).astype(BF16)
+    v_out[...] = mm(encoder[...], matrix(2)).astype(BF16)
     attend(q_out[...], k_out[...], v_out[...], allowed, None, probs, attn)
-    result = values + live * mm(attn[...], whole(weights, 3))
+    result = values + live * mm(attn[...], matrix(3))
     hidden[...] = result
     normed_out[...] = rms_parts(result, gain_next[...])[1]
 
@@ -255,11 +265,12 @@
             ]
 
 
-def feed_forward(last, seq_count, info, normed_ref, cotangent, mine, theirs, *refs):
+def feed_forward(last, seq_count, info, normed_ref, cotangent, mine_ref, theirs_ref, *refs):
+    *refs, mine, theirs, g_mine, g_other, sems, out_sems = refs
     if last:
-        hidden, gain, total, back, mixed, grad_hidden, grad_gain, g_mine, g_other = refs
+        hidden, gain, total, back, mixed, grad_hidden, grad_gain, g_mine_ref, g_other_ref = refs
     else:
-        total_out, back_out, g_mine, g_other = refs
+        total_out, back_out, g_mine_ref, g_other_ref = refs
     flag = info[0] == 0
     rows, width = cotangent.shape
     half = width // 2
@@ -268,9 +279,28 @@
     units = wide // count
     owners = max(1, 256 // units)
     chunk = owners * units
+
+    def parts(step, left, right, flags):
+        lanes = pl.ds(step * chunk, chunk)
+        places = pl.ds(step * owners, owners)
+        copies = []
+        for source, target in zip(left, right):
+            for where in ((slice(None), slice(None), lanes), (places, slice(None), pl.ds(wide, packed - wide))):
+                copies.append(
+                    pltpu.make_async_copy(source.at[where], target.at[where], flags.at[step, len(copies)])
+                )
+        return copies
+
+    steps = range(wide // chunk)
+    coming = [parts(step, (mine_ref, theirs_ref), (mine, theirs), sems) for step in steps]
+    for copies in coming:
+        for copy in copies:
+            copy.start()
+    going = [parts(step, (g_mine, g_other), (g_mine_ref, g_other_ref), out_sems) for step in steps]
     bounds = read_bounds(info, seq_count)
     live = (segments(bounds, (rows, 1), 0) < seq_count).astype(F32)
     normed = normed_ref[...]
+    normed_t = normed.T
     branch = (live * cotangent[...].astype(F32)).astype(BF16)
     left, right = branch[:, :half], branch[:, half:]
     b_mine, b_other = choose(flag, left, right), choose(flag, right, left)
@@ -280,7 +310,9 @@
         sum_mine = jnp.zeros((rows, half), F32)
         sum_other = jnp.zeros((rows, half), F32)
         sum_back = jnp.zeros((rows, width), F32)
-    for step in range(wide // chunk):
+    for step in steps:
+        for copy in coming[step]:
+            copy.wait()
         lanes = slice(step * chunk, (step + 1) * chunk)
         places = range(step * owners, (step + 1) * owners)
         own = mine[:, :, lanes].reshape(width, chunk)
@@ -303,14 +335,17 @@
         d_up = (d_act * gelu).astype(BF16)
         d_own, d_other = choose(flag, d_gate, d_up), choose(flag, d_up, d_gate)
         sum_back += mm_nt(d_own, own) + mm_nt(d_other, other)
-        g_mine[:, :, lanes] = mm_tn(normed, d_own).astype(BF16).reshape(count, -1, chunk)
-        g_other[:, :, lanes] = mm_tn(normed, d_other).astype(BF16).reshape(count, -1, chunk)
-        down_grad = mm_tn(act, b_mine).astype(BF16)
-        down_grad_other = mm_tn(act, b_other).astype(BF16)
+        g_mine[:, :, lanes] = mm(normed_t, d_own).astype(BF16).reshape(count, -1, chunk)
+        g_other[:, :, lanes] = mm(normed_t, d_other).astype(BF16).reshape(count, -1, chunk)
+        act_t = act.T
+        down_grad = mm(act_t, b_mine).astype(BF16)
+        down_grad_other = mm(act_t, b_other).astype(BF16)
         for index, owner in enumerate(places):
             here = slice(index * units, (index + 1) * units)
             pack_down(g_mine, owner, wide, down_grad[here])
             pack_down(g_other, owner, wide, down_grad_other[here])
+        for copy in going[step]:
+            copy.start()
     if last:
         outcome = jnp.concatenate(
             [choose(flag, sum_mine, sum_other), choose(flag, sum_other, sum_mine)], axis=1
@@ -323,41 +358,45 @@
         total_out[0] = sum_mine
         total_out[1] = sum_other
         back_out[...] = sum_back
+    for copies in going:
+        for copy in copies:
+            copy.wait()
 
 
 def cross_backward(
     seq_count, info, grad_in, hidden_one, gain, encoder, queries, keys, values, probs, attn, mine, theirs,
-    grad_out, grad_enc, grad_gain, g_own, g_side, g_core, g_far, weights, grads, lefts, sems,
+    grad_out, grad_enc, grad_gain, g_own, g_side, g_core, g_far, g_far_two, weights, grads, held, sems, out_sems,
 ):
-    copies = load_weights(info, mine, theirs, weights, sems)
+    matrix = Weights(info, mine, theirs, weights, sems, (3, 0, 1, 2))
     rows = hidden_one.shape[0]
     bounds = read_bounds(info, seq_count)
     live = (segments(bounds, (rows, 1), 0) < seq_count).astype(F32)
     grad = grad_in[...]
     branch = (live * grad).astype(BF16)
     _, normed = rms_parts(hidden_one[...], gain[...])
-    lefts[0] = normed
-    lefts[1] = encoder[...]
-    lefts[2] = encoder[...]
-    lefts[3] = attn[...]
     grads[3] = branch
+    normed_t, encoder_t, attn_t = normed.T, encoder[...].T, attn[...].T
+
+    def lefts(place):
+        return choose(place == 0, normed_t, choose(place == 3, attn_t, encoder_t))
+
+    grad_attn = mm_nt(branch, matrix(3)).astype(BF16)
+    attend_back(queries[...], keys[...], values[...], grad_attn, probs, grads.at[0], grads.at[1], grads.at[2], None)
+    copies = weight_grads(info, lefts, grads, held, (g_own, g_side, g_core, g_far, g_far_two), out_sems)
+    d_query, d_key, d_value = grads[0], grads[1], grads[2]
+    grad_enc[...] = mm_nt(d_key, matrix(1)) + mm_nt(d_value, matrix(2))
+    part, term = rms_back(hidden_one[...], gain[...], mm_nt(d_query, matrix(0)))
+    grad_out[...] = grad + part
+    grad_gain[...] = term
     for copy in copies:
         copy.wait()
-    grad_attn = mm_nt(branch, whole(weights, 3)).astype(BF16)
-    attend_back(queries[...], keys[...], values[...], grad_attn, probs, grads.at[0], grads.at[1], grads.at[2], None)
-    weight_grads(info, lefts, grads, (g_own, g_side, g_core, g_far))
-    d_query, d_key, d_value = grads[0], grads[1], grads[2]
-    grad_enc[...] = mm_nt(d_key, whole(weights, 1)) + mm_nt(d_value, whole(weights, 2))
-    part, term = rms_back(hidden_one[...], gain[...], mm_nt(d_query, whole(weights, 0)))
-    grad_out[...] = grad + part
-    grad_gain[...] = term
 
 
 def self_backward(
     seq_count, info, grad_in, tokens, gain, queries, keys, values, probs, attn, mine, theirs,
-    grad_out, grad_gain, grad_line, g_own, g_side, g_core, g_far, weights, grads, sems,
+    grad_out, grad_gain, grad_line, g_own, g_side, g_core, g_far, g_far_two, weights, grads, held, sems, out_sems,
 ):
-    copies = load_weights(info, mine, theirs, weights, sems)
+    matrix = Weights(info, mine, theirs, weights, sems, (3, 0, 1, 2))
     rows = tokens.shape[0]
     bounds = read_bounds(info, seq_count)
     live = (segments(bounds, (rows, 1), 0) < seq_count).astype(F32)
@@ -374,20 +413,62 @@
         turned = pltpu.roll(mm(flip, score), 1, 1, stride=1, stride_axis=0)
         grad_line[head : head + 1, :] = jnp.sum(turned, axis=0, keepdims=True)
 
-    for copy in copies:
-        copy.wait()
-    grad_attn = mm_nt(branch, whole(weights, 3)).astype(BF16)
+    grad_attn = mm_nt(branch, matrix(3)).astype(BF16)
     attend_back(
         queries[...], keys[...], values[...], grad_attn, probs, grads.at[0], grads.at[1], grads.at[2], collect
     )
-    weight_grads(info, (normed, attn[...]), grads, (g_own, g_side, g_core, g_far))
+    normed_t, attn_t = normed.T, attn[...].T
+    copies = weight_grads(
+        info,
+        lambda place: choose(place == 3, attn_t, normed_t),
+        grads,
+        held,
+        (g_own, g_side, g_core, g_far, g_far_two),
+        out_sems,
+    )
     d_query, d_key, d_value = grads[0], grads[1], grads[2]
     grad_normed = (
-        mm_nt(d_query, whole(weights, 0)) + mm_nt(d_key, whole(weights, 1)) + mm_nt(d_value, whole(weights, 2))
+        mm_nt(d_query, matrix(0)) + mm_nt(d_key, matrix(1)) + mm_nt(d_value, matrix(2))
     )
     part, term = rms_back(inputs, gain[...], grad_normed)
     grad_out[...] = grad + part
     grad_gain[...] = term
+    for copy in copies:
+        copy.wait()
+
+
+def finish_quarters(info, own, across, core, far, *outs):
+    for place, out in enumerate(outs):
+        same_core, same_side = info[0] == place // 2, info[3] == place % 2
+        near = choose(same_side, own[...], across[...])
+        out[...] = choose(same_core, near, choose(same_side, core[...], far[...])).astype(F32)
+
+
+def finish_feed(info, one, two, there_one, there_two, gate, up, down):
+    core_zero, side_zero = info[0] == 0, info[3] == 0
+    rows, packed = one.shape
+    wide = packed * 2 // 3
+    units = down.shape[0] // 2
+    half = down.shape[1] // 2
+    sub = rows // 3
+    pairs = ((one[...], there_one[...]), (two[...], there_two[...]))
+    for part in range(2):
+        first, second = pairs[part], pairs[1 - part]
+        here, there = (choose(side_zero, first[k], second[k]) for k in range(2))
+        for values, target, column in (
+            (choose(core_zero, here, there), gate, 0),
+            (choose(core_zero, there, here), up, half),
+        ):
+            values = values.astype(F32)
+            for owner in range(wide // units):
+                start = (2 * owner + part) * units
+                target[:, start : start + units] = values[:, owner * units : (owner + 1) * units]
+            for i in range(4):
+                for g in range(3):
+                    down[
+                        part * units + sub * i : part * units + sub * (i + 1),
+                        column + PAIR * g : column + PAIR * (g + 1),
+                    ] = values[sub * g : sub * (g + 1), wide + PAIR * i : wide + PAIR * (i + 1)]
 
 
 class Links:
@@ -418,56 +499,53 @@
             functools.partial(collect_kernel, self.high),
             out_shape=jax.ShapeDtypeStruct((self.count,) + local.shape, local.dtype),
             in_specs=[SMEM] + [ANY] * len(pieces),
-            out_specs=ANY,
+            out_specs=VMEM,
             scratch_shapes=[pltpu.SemaphoreType.DMA((len(pieces),))],
             compiler_params=params(16),
             cost_estimate=cost(0, nbytes),
         )(info, *pieces)
 
-    def gather(self, locals_, window):
-        got, sent, order = {}, [], []
-        for index, local in enumerate(locals_):
-            got[index, 0, 0] = local
-            ring = []
-            bit = self.high // 2
+    def order(self, buckets):
+        if self.high == 4 and buckets == 3:
+            plan = "H02 L00 H01 L10 H03 L01 L02 H12 L20 L03 H11 H13 L11 L12 H22 L13 H21 L21 H23 L22 L23"
+            steps = [(step[0] == "H", int(step[1]), int(step[2])) for step in plan.split()]
+        else:
             keys = [0]
-            while bit:
-                for key in list(keys):
-                    keys.append(key | bit)
-                    ring.append(((index, key, 0), (index, key | bit, 0), bit))
-                bit //= 2
-            side = [((index, key, 0), (index, key, 1), 0) for key in keys]
-            order.append((ring, side))
-        queue, pending = [], []
-        for ring, side in order:
-            side = list(side)
-            for item in ring:
-                queue.append(item)
-                if pending:
-                    queue.append(pending.pop(0))
-                elif side:
-                    queue.append(side.pop(0))
-            pending += side
-        queue += pending
-        ready = set((i, 0, 0) for i in range(len(locals_)))
-        waiting = list(queue)
+            while len(keys) < self.high:
+                keys += [key | (self.high // (2 * len(keys))) for key in keys]
+            steps = [(lane, index, key) for index in range(buckets) for key in keys for lane in (True, False)]
+            steps = [step for step in steps if not step[0] or step[2]]
         queue = []
-        while waiting:
-            place = next(i for i, item in enumerate(waiting) if item[0] in ready)
-            item = waiting.pop(place)
-            ready.add(item[1])
-            queue.append(item)
+        for lane, index, key in steps:
+            bit = key & -key
+            if lane:
+                queue.append(((index, key ^ bit, 0), (index, key, 0), bit))
+            else:
+                queue.append(((index, key, 0), (index, key, 1), 0))
+        return queue
+
+    def gather(self, locals_, window, hooks):
+        got = {(index, 0, 0): local for index, local in enumerate(locals_)}
+        queue = self.order(len(locals_))
+        lasts = {index: max(n for n, item in enumerate(queue) if item[0][0] == index) for index in range(len(locals_))}
+        hooks = {min(lasts[index] + lag, len(queue) - 2): (index, function) for index, lag, function in hooks}
+        token = None
         for number, (source, target, bit) in enumerate(queue):
             values = got[source]
+            if token is not None:
+                values, token = after(values, token)[0], None
             if number >= window:
                 old = queue[number - window][1]
                 if old != source:
                     values, got[old] = lax.optimization_barrier((values, got[old]))
             got[target] = self.swap_high(values, bit) if bit else self.swap_low(values)
-        return [
-            [got[index, key, side] for key in range(self.high) for side in range(2)]
-            for index in range(len(locals_))
-        ]
+            if number in hooks:
+                index, function = hooks[number]
+                token = function(self.pieces(got, index))
+        return [self.pieces(got, index) for index in range(len(locals_))]
+
+    def pieces(self, got, index):
+        return [got[index, key, side] for key in range(self.high) for side in range(2)]
 
     def split(self, values):
         values = values.reshape((self.high, 2) + values.shape[1:])
@@ -600,12 +678,11 @@
         [jnp.where(core_zero, q_cross, v_cross), jnp.where(core_zero, k_cross, o_cross)]
     )
     feed_pieces, first_pieces, second_pieces = comm.gather(
-        [feed_local, first_local, second_local], 4
-    )
-    feed_one = comm.collect(info, feed_pieces)
+        [feed_local, first_local, second_local], 4, []
+    )
+    feed_one, first_mine = comm.collect(info, feed_pieces), comm.collect(info, first_pieces)
     feed_two = comm.swap_replica(feed_one, 2)
     feed_one_theirs = comm.swap_replica(feed_one, 1)
-    first_mine = comm.collect(info, first_pieces)
     first_theirs = comm.swap_replica(first_mine, 1)
 
     vectors = first_mine[:, 2 * rows, :small_count].astype(F32)
@@ -658,20 +735,24 @@
     )(info, hidden_one, gain_two, gain_three, encoder, second_mine, second_theirs)
 
     packed = shape(*feed_one.shape)
+    feed_steps = pltpu.SemaphoreType.DMA((count, 4))
+    feed_scratch = [pltpu.VMEM(feed_one.shape, BF16)] * 4 + [feed_steps, feed_steps]
     feed_cost = cost(9 * row_count * width * hidden_units, 12 * width * hidden_units)
     total, back, g_one, g_one_other = pl.pallas_call(
         functools.partial(feed_forward, False, seq_count),
         out_shape=(shape(2, row_count, half, dtype=F32), act32, packed, packed),
-        in_specs=[SMEM] + [VMEM] * 4,
-        out_specs=[VMEM] * 4,
+        in_specs=[SMEM, VMEM, VMEM, ANY, ANY],
+        out_specs=[VMEM, VMEM, ANY, ANY],
+        scratch_shapes=feed_scratch,
         compiler_params=params(),
         cost_estimate=feed_cost,
     )(info, normed_three, cotangent[0], feed_one, feed_one_theirs)
     mixed, grad_hidden_two, grad_norm_three, g_two, g_two_other = pl.pallas_call(
         functools.partial(feed_forward, True, seq_count),
         out_shape=(act, act32, vec32, packed, packed),
-        in_specs=[SMEM] + [VMEM] * 8,
-        out_specs=[VMEM] * 5,
+        in_specs=[SMEM, VMEM, VMEM, ANY, ANY] + [VMEM] * 4,
+        out_specs=[VMEM] * 3 + [ANY] * 2,
+        scratch_shapes=feed_scratch,
         compiler_params=params(),
         cost_estimate=feed_cost,
     )(info, normed_three, cotangent[0], feed_two, feed_two_theirs, hidden_two, gain_three, total, back)
@@ -684,24 +765,27 @@
     grad_hidden_two = sequence(grad_hidden_two)
 
     grads = shape(count, rows, width)
+    grads_half = shape(count // 2, rows, width)
+    out_sems = pltpu.SemaphoreType.DMA((5,))
     grad_hidden_one, grad_encoder, grad_norm_two, *g_second = pl.pallas_call(
         functools.partial(cross_backward, seq_count),
-        out_shape=(act32, shape(enc_rows, width, dtype=F32), vec32) + (grads,) * 4,
+        out_shape=(act32, shape(enc_rows, width, dtype=F32), vec32) + (grads,) * 3 + (grads_half,) * 2,
         in_specs=[SMEM] + [VMEM] * 9 + [ANY] * 2,
-        out_specs=[VMEM] * 7,
-        scratch_shapes=[weight_scratch, attn_scratch, attn_scratch, sems],
+        out_specs=[VMEM] * 3 + [ANY] * 5,
+        scratch_shapes=[weight_scratch, attn_scratch, weight_scratch, sems, out_sems],
         compiler_params=params(),
         cost_estimate=cost(10 * pair_flops, 2 * weight_bytes),
     )(
         info, grad_hidden_two, hidden_one, gain_two, encoder, queries_c, keys_c, values_c, probs_c, attn_two,
         second_mine, second_theirs,
     )
-    def across(g_own, g_side, g_core, g_far):
-        from_far = comm.swap_replica(g_far, 1)
+    def across(g_own, g_side, g_core, *g_far):
+        from_far = [comm.swap_replica(part, 1) for part in g_far]
         from_core = comm.swap_replica(g_core, 1)
 
         def finish():
-            side = sequence.mark(add(sequence(from_far), g_side))
+            from_far[0] = sequence(from_far[0])
+            side = sequence.mark(add(jnp.concatenate(from_far), g_side))
             return g_own, from_core, comm.swap_replica(side, 2)
 
         return finish
@@ -713,10 +797,10 @@
 
     grad_inputs, grad_norm_one, grad_line, *g_first = pl.pallas_call(
         functools.partial(self_backward, seq_count),
-        out_shape=(act32, vec32, shape(16, row_count, dtype=F32)) + (grads,) * 4,
+        out_shape=(act32, vec32, shape(16, row_count, dtype=F32)) + (grads,) * 3 + (grads_half,) * 2,
         in_specs=[SMEM] + [VMEM] * 8 + [ANY] * 2,
-        out_specs=[VMEM] * 7,
-        scratch_shapes=[weight_scratch, attn_scratch, sems],
+        out_specs=[VMEM] * 3 + [ANY] * 5,
+        scratch_shapes=[weight_scratch, attn_scratch, weight_scratch, sems, out_sems],
         compiler_params=params(),
         cost_estimate=cost(10 * pair_flops, 2 * weight_bytes),
     )(
@@ -726,8 +810,8 @@
     sequence.mark(grad_norm_one)
     first_across = across(*g_first)
     one.step()
+    first_parts = first_across()
     second.low(*second_parts)
-    first_parts = first_across()
     grad_table = jnp.dot(grad_line[:HEADS], bucket_hot, precision=lax.Precision.HIGHEST).T
     table_row = jnp.pad(grad_table.reshape(1, -1), ((0, 0), (0, width - grad_table.size)))
     vectors = jnp.concatenate([grad_norm_one, grad_norm_two, grad_norm_three, table_row])
@@ -774,43 +858,61 @@
     first_sum = first.over_replicas(first.finish(), 4)
     first_cross, first_core = comm.swap_replica(first_sum, 2), comm.swap_replica(first_sum, 1)
     second_far = comm.swap_replica(second_cross, 1)
-    first_far = comm.swap_replica(first_cross, 1)
-
-    def four(own, across, core, far):
-        zero, one = jnp.where(side_zero, own, across), jnp.where(side_zero, across, own)
-        two, three = jnp.where(side_zero, core, far), jnp.where(side_zero, far, core)
-        return [
-            jnp.where(core_zero, left, right).astype(F32)
-            for left, right in ((zero, two), (one, three), (two, zero), (three, one))
-        ]
+    first_far = None
+
+    full = jax.ShapeDtypeStruct((rows, width), F32)
+
+    def four(*arrays):
+        return pl.pallas_call(
+            finish_quarters,
+            out_shape=(full,) * 4,
+            in_specs=[SMEM] + [VMEM] * 4,
+            out_specs=[VMEM] * 4,
+            compiler_params=params(16),
+            cost_estimate=cost(0, 24 * rows * width),
+        )(info, *arrays)
 
     owned = lax.dynamic_slice(vectors, (0, comm.place * rows), (3, rows))
     table_size = bias_table.size
     owned_table = lax.dynamic_slice(vectors[3], (comm.place * table_size,), (table_size,))
 
     second = four(second_sum, second_cross, second_core, second_far)
-    def by_side(one, two):
-        return jnp.where(side_zero, one, two), jnp.where(side_zero, two, one)
-
-    here, there = by_side(one_sum, two_sum), by_side(*there)
-    wide_units = hidden_units // 2
-
-    def wide_grad(parts):
-        parts = [part[:, :wide_units].reshape(rows, count, 1, units) for part in parts]
-        return jnp.concatenate(parts, axis=2).reshape(rows, hidden_units).astype(F32)
-
-    def down_grad(parts):
-        parts = [
-            part[:, wide_units:].reshape(3, units // 4, 4, PAIR).transpose(2, 1, 0, 3).reshape(units, half)
-            for part in parts
-        ]
-        return jnp.concatenate(parts, axis=0)
-
-    low = [jnp.where(core_zero, one, two) for one, two in zip(here, there)]
-    high = [jnp.where(core_zero, two, one) for one, two in zip(here, there)]
-    grad_down = jnp.concatenate([down_grad(low), down_grad(high)], axis=1).astype(F32)
-    grad_gate, grad_up = wide_grad(low), wide_grad(high)
-    first = four(first_sum, first_cross, after(first_core, grad_gate, grad_up, grad_down, *second)[0], first_far)
+    if units % PAIR == 0:
+        grad_gate, grad_up, grad_down = pl.pallas_call(
+            finish_feed,
+            out_shape=(
+                shape(rows, hidden_units, dtype=F32), shape(rows, hidden_units, dtype=F32),
+                shape(down_rows, width, dtype=F32),
+            ),
+            in_specs=[SMEM] + [VMEM] * 4,
+            out_specs=[VMEM] * 3,
+            compiler_params=params(16),
+            cost_estimate=cost(0, 36 * rows * hidden_units),
+        )(info, one_sum, two_sum, *there)
+    else:
+        def by_side(one, two):
+            return jnp.where(side_zero, one, two), jnp.where(side_zero, two, one)
+
+        here, there = by_side(one_sum, two_sum), by_side(*there)
+        wide_units = hidden_units // 2
+
+        def wide_grad(parts):
+            parts = [part[:, :wide_units].reshape(rows, count, 1, units) for part in parts]
+            return jnp.concatenate(parts, axis=2).reshape(rows, hidden_units).astype(F32)
+
+        def down_grad(parts):
+            parts = [
+                part[:, wide_units:].reshape(3, units // 4, 4, PAIR).transpose(2, 1, 0, 3).reshape(units, half)
+                for part in parts
+            ]
+            return jnp.concatenate(parts, axis=0)
+
+        low = [jnp.where(core_zero, one, two) for one, two in zip(here, there)]
+        high = [jnp.where(core_zero, two, one) for one, two in zip(here, there)]
+        grad_down = jnp.concatenate([down_grad(low), down_grad(high)], axis=1).astype(F32)
+        grad_gate, grad_up = wide_grad(low), wide_grad(high)
+    first_far = comm.swap_replica(after(first_cross, grad_gate, grad_up, grad_down, *second)[0], 1)
+    first = four(first_sum, first_cross, first_core, first_far)
     return (
         mixed[None],
         grad_inputs[None],

time: 286 us -> 267 us (0.934)
  starting transfers between devices: 57.5 us -> 38.3 us
  waiting for transfers between devices: 120 us -> 130 us
  other arithmetic: 31.2 us -> 21.3 us
  Pallas kernels: 58 us -> 65.6 us
  local copies, waits for them, and re-layouts: 12.5 us -> 8.41 us
    ppermute x17, starting transfers between devices: 23 us -> 12.8 us  [swap_high(): lax.ppermute(values, 'fsdp', [(i, i ^ 2 * step) for i in range(self.count)])]
    ppermute x17, waiting for transfers between devices: 63.7 us -> 71.3 us  [swap_high(): lax.ppermute(values, 'fsdp', [(i, i ^ 2 * step) for i in range(self.count)])]
    convert_element_type x5 -> x0, other arithmetic: 7.18 us -> none  [the longest x2 4.42 us: four(): jnp.where(core_zero, left, right).astype(F32)]
    ppermute x5, waiting for transfers between devices: 8.81 us -> 2.56 us  [small_step(): lax.ppermute(sequence(vectors), axis, [(i, i ^ bit) for i in range(size)])]
    ppermute x23 -> x25, waiting for transfers between devices: 4.55 us -> 10.8 us  [swap_replica(): return lax.ppermute(values, 'replica', pairs)]
    pallas_call x0 -> x3, Pallas kernels: none -> 5.3 us  [the longest x2 3.2 us: four(): pl.pallas_call(finish_quarters, out_shape=(full,) * 4, in_specs=[SMEM] +...]
    ppermute x16, starting transfers between devices: 19 us -> 14.4 us  [swap_low(): return lax.ppermute(values, 'fsdp', [(i, i ^ 1) for i in range(self.count)])]
    convert_element_type x2 -> x0, local copies, waits for them, and re-layouts: 3.02 us -> none  [wide_grad(): jnp.concatenate(parts, axis=2).reshape(rows, hidden_units).astype(F32)]
  transfers between devices with their start and end apart: 61 -> 63, of which waited for: 27 -> 31; matrix products, arithmetic and copies ran while one was open for 14% -> 10% of each run, Pallas kernels for 21% -> 23%
where the time goes in v1:
time: 267 us; the launch traced here: 266 us
  waiting for transfers between devices  130 us (49%)
  Pallas kernels  65.6 us (25%)
  starting transfers between devices  38.3 us (14%)
  other arithmetic  21.3 us (8%)
  local copies, waits for them, and re-layouts  8.41 us (3%)
    ppermute x17, waiting for transfers between devices, swap_high(): lax.ppermute(values, 'fsdp', [(i, i ^ 2 * step) for i in range(self.count)])  71.3 us
    ppermute x16, waiting for transfers between devices, swap_low(): return lax.ppermute(values, 'fsdp', [(i, i ^ 1) for i in range(self.count)])  45.3 us
    convert_element_type x19, other arithmetic, add(): functools.reduce(jnp.add, [term.astype(F32) for term in terms]).astype(BF16)  18.8 us
    ppermute x16, starting transfers between devices, swap_low(): return lax.ppermute(values, 'fsdp', [(i, i ^ 1) for i in range(self.count)])  14.4 us
    ppermute x17, starting transfers between devices, swap_high(): lax.ppermute(values, 'fsdp', [(i, i ^ 2 * step) for i in range(self.count)])  12.8 us
    pallas_call x1, Pallas kernels, per_device(): pl.pallas_call(functools.partial(feed_forward, True, seq_count), out_shap...  11.1 us
    ppermute x25, waiting for transfers between devices, swap_replica(): return lax.ppermute(values, 'replica', pairs)  10.8 us
    pallas_call x1, Pallas kernels, per_device(): pl.pallas_call(functools.partial(feed_forward, False, seq_count), out_sha...  10.1 us
  transfers between devices with their start and end apart: 63, of which 31 were waited for; matrix products, arithmetic and copies ran while one was open for 10% of the time, Pallas kernels for 23%

profile of v1, /device:TPU:0, one launch (start us, length us, event | category | flops | bytes accessed | tf_op | source)
XLA Modules:
  0.0 266.2 jit_solution(14747186686734825342)
XLA Ops:
  14.5 6.8 %collective-permute-done.2.refs_2_ = bf16[96,1536]{1,0:T(8,128)(2,1)S(1)} collective-permute-done((bf16[96,1536]{1,0:T(8,128)(2,1)S(1)}, bf16[96,1536]{1,0:T(8,128)(2,1)S(1)}, u32[]{:S(2)}, u32[]{:S(2)}) %collective-permute-start.2) | collective-permute-done | bytes 294944 | tf_op jit(solution)/shard_map/ppermute | solution.py:493
  27.5 6.6 %collective-permute-done.5.refs_6_ = bf16[96,1536]{1,0:T(8,128)(2,1)S(1)} collective-permute-done((bf16[96,1536]{1,0:T(8,128)(2,1)S(1)}, bf16[96,1536]{1,0:T(8,128)(2,1)S(1)}, u32[]{:S(2)}, u32[]{:S(2)}) %collective-permute-start.5) | collective-permute-done | bytes 294944 | tf_op jit(solution)/shard_map/ppermute | solution.py:493
  37.4 3.3 %collective-permute-done.8.refs_4_ = bf16[208,768]{1,0:T(8,128)(2,1)S(1)} collective-permute-done((bf16[208,768]{1,0:T(8,128)(2,1)S(1)}, bf16[208,768]{1,0:T(8,128)(2,1)S(1)}, u32[]{:S(2)}, u32[]{:S(2)}) %collective-permute-start.8) | collective-permute-done | bytes 319520 | tf_op jit(solution)/shard_map/ppermute | solution.py:493
  41.7 3.5 %shard_map.344.mine_ref = bf16[8,96,1536]{2,1,0:T(8,128)(2,1)} custom-call(s32[6]{0:T(128)S(1)} %concatenate.24.info, bf16[96,1536]{1,0:T(8,128)(2,1)S(1)} %bitcast_dynamic-update-slice_fusion.1.refs_0_, bf16[96,1536]{1,0:T(8,128)(2,1)S(1)} %collective-permute-done.10.refs_1_, bf16[96,1536]{1,0:T(8,128)(2,1)S(1)} %collective-permute-done.2.refs_2_, ...), custom_call_target="tpu_custom_call" | custom-call | bytes 4718592 | tf_op jit(solution)/shard_map/pallas_call | solution.py:498
  49.3 4.5 %collective-permute-done.6.refs_1_ = bf16[192,768]{1,0:T(8,128)(2,1)S(1)} collective-permute-done((bf16[192,768]{1,0:T(8,128)(2,1)S(1)}, bf16[192,768]{1,0:T(8,128)(2,1)S(1)}, u32[]{:S(2)}, u32[]{:S(2)}) %collective-permute-start.6) | collective-permute-done | bytes 294944 | tf_op jit(solution)/shard_map/ppermute | solution.py:490
  53.8 6.6 %collective-permute-done.4.refs_2_ = bf16[208,768]{1,0:T(8,128)(2,1)S(1)} collective-permute-done((bf16[208,768]{1,0:T(8,128)(2,1)S(1)}, bf16[208,768]{1,0:T(8,128)(2,1)S(1)}, u32[]{:S(2)}, u32[]{:S(2)}) %collective-permute-start.4) | collective-permute-done | bytes 319520 | tf_op jit(solution)/shard_map/ppermute | solution.py:493
  65.8 4.9 %collective-permute-done.15.refs_4_ = bf16[192,768]{1,0:T(8,128)(2,1)S(1)} collective-permute-done((bf16[192,768]{1,0:T(8,128)(2,1)S(1)}, bf16[192,768]{1,0:T(8,128)(2,1)S(1)}, u32[]{:S(2)}, u32[]{:S(2)}) %collective-permute-start.15) | collective-permute-done | bytes 294944 | tf_op jit(solution)/shard_map/ppermute | solution.py:493
  72.7 4.9 %collective-permute-done.16.refs_7_ = bf16[208,768]{1,0:T(8,128)(2,1)S(1)} collective-permute-done((bf16[208,768]{1,0:T(8,128)(2,1)S(1)}, bf16[208,768]{1,0:T(8,128)(2,1)S(1)}, u32[]{:S(2)}, u32[]{:S(2)}) %collective-permute-start.16) | collective-permute-done | bytes 319520 | tf_op jit(solution)/shard_map/ppermute | solution.py:490
  87.2 3.5 %collective-permute-done.20.refs_5_ = bf16[192,768]{1,0:T(8,128)(2,1)S(1)} collective-permute-done((bf16[192,768]{1,0:T(8,128)(2,1)S(1)}, bf16[192,768]{1,0:T(8,128)(2,1)S(1)}, u32[]{:S(2)}, u32[]{:S(2)}) %collective-permute-start.20) | collective-permute-done | bytes 294944 | tf_op jit(solution)/shard_map/ppermute | solution.py:490
  90.7 5.3 %collective-permute-done.21.refs_7_ = bf16[192,768]{1,0:T(8,128)(2,1)S(1)} collective-permute-done((bf16[192,768]{1,0:T(8,128)(2,1)S(1)}, bf16[192,768]{1,0:T(8,128)(2,1)S(1)}, u32[]{:S(2)}, u32[]{:S(2)}) %collective-permute-start.21) | collective-permute-done | bytes 294944 | tf_op jit(solution)/shard_map/ppermute | solution.py:490
  105.8 5.8 %shard_map.341 = (bf16[128,768]{1,0:T(8,128)(2,1)}, bf16[128,768]{1,0:T(8,128)(2,1)}, bf16[128,768]{1,0:T(8,128)(2,1)}, f32[12,128,128]{2,1,0:T(8,128)}, bf16[128,768]{1,0:T(8,128)(2,1)}, /*index=5*/f32[128,768]{1,0:T(8,128)}) custom-call(s32[6]{0:T(128)} %copy-done.5, bf16[128,768]{1,0:T(8,128)(2,1)} %bitcast.144, f32[1,768]{1,0:T(1,128)} %reshape.189.gain, ...), custom_call_target="tpu_custom_call" | custom-call | flops 754974720 | bytes 4718592 | tf_op jit(solution)/shard_map/pallas_call | solution.py:714
  111.6 5.7 %shard_map.343 = (bf16[128,768]{1,0:T(8,128)(2,1)}, bf16[128,768]{1,0:T(8,128)(2,1)}, bf16[128,768]{1,0:T(8,128)(2,1)}, f32[12,128,128]{2,1,0:T(8,128)}, bf16[12...) custom-call(s32[6]{0:T(128)} %copy-done.5, f32[128,768]{1,0:T(8,128)} %get-tuple-element.141.hidden_one, ...), custom_call_target="tpu_custom_call" | custom-call | flops 754974720 | bytes 4718592 | tf_op jit(solution)/shard_map/pallas_call | solution.py:727
  117.3 10.1 %shard_map.345 = (f32[2,128,384]{2,1,0:T(8,128)}, f32[128,768]{1,0:T(8,128)}, bf16[8,96,1536]{2,1,0:T(8,128)(2,1)}, bf16[8,96,1536]{2,1,0:T(8,128)(2,1)}) custom-call(s32[6]{0:T(128)} %copy-done.5, bf16[128,768]{1,0:T(8,128)(2,1)} %get-tuple-element.147.normed_ref, bf16[128,768]{1,0:T(8,128)(2,1)} %bitcast.154, bf16[8,96,1536]{2,1,0:T(8,128)(2,1)} %shard_map.344.mine_ref, ...), custom_call_target="tpu_custom_call" | custom-call | flops 1811939328 | bytes 18874368 | tf_op jit(solution)/shard_map/pallas_call | solution.py:741
  127.9 11.1 %shard_map.346 = (bf16[128,768]{1,0:T(8,128)(2,1)}, f32[128,768]{1,0:T(8,128)}, f32[1,768]{1,0:T(1,128)}, bf16[8,96,1536]{2,1,0:T(8,128)(2,1)}, bf16[8,96,1536]{2,1,0:T(8,128)(2,1)}) custom-call(s32[6]{0:T(128)} %copy-done.5, bf16[128,768]{1,0:T(8,128)(2,1)} %get-tuple-element.147.normed_ref, bf16[128,768]{1,0:T(8,128)(2,1)} %bitcast.155, ...), custom_call_target="tpu_custom_call" | custom-call | flops 1811939328 | bytes 18874368 | tf_op jit(solution)/shard_map/pallas_call | solution.py:750
  142.0 10.0 %shard_map.347 = (f32[128,768]{1,0:T(8,128)}, f32[128,768]{1,0:T(8,128)}, f32[1,768]{1,0:T(1,128)}, bf16[8,96,768]{2,1,0:T(8,128)(2,1)}, bf16[8,96,768]{2,1,0:T(...) custom-call(s32[6]{0:T(128)} %copy-done.5, ...), custom_call_target="tpu_custom_call" | custom-call | flops 1509949440 | bytes 9437184 | tf_op jit(solution)/shard_map/pallas_call | solution.py:770
  159.0 10.0 %shard_map.348 = (f32[128,768]{1,0:T(8,128)}, f32[1,768]{1,0:T(1,128)}, f32[16,128]{1,0:T(8,128)}, bf16[8,96,768]{2,1,0:T(8,128)(2,1)}, bf16[8,96,768]{2,1,0:T(8...) custom-call(s32[6]{0:T(128)} %copy-done.5, ...), custom_call_target="tpu_custom_call" | custom-call | flops 1509949440 | bytes 9437184 | tf_op jit(solution)/shard_map/pallas_call | solution.py:798
  179.1 8.6 %collective-permute-done.34 = bf16[8,96,768]{2,1,0:T(8,128)(2,1)} collective-permute-done((bf16[8,96,768]{2,1,0:T(8,128)(2,1)}, bf16[8,96,768]{2,1,0:T(8,128)(2,1)}, u32[]{:S(2)}, u32[]{:S(2)}) %collective-permute-start.34) | collective-permute-done | bytes 1179680 | tf_op jit(solution)/shard_map/ppermute | solution.py:487
  191.0 5.1 %collective-permute-done.36 = bf16[4,96,1536]{2,1,0:T(8,128)(2,1)} collective-permute-done((bf16[4,96,1536]{2,1,0:T(8,128)(2,1)}, bf16[4,96,1536]{2,1,0:T(8,128)(2,1)}, u32[]{:S(2)}, u32[]{:S(2)}) %collective-permute-start.36) | collective-permute-done | bytes 1179680 | tf_op jit(solution)/shard_map/ppermute | solution.py:490
  199.5 8.7 %collective-permute-done.39 = bf16[4,96,768]{2,1,0:T(8,128)(2,1)S(1)} collective-permute-done((bf16[4,96,768]{2,1,0:T(8,128)(2,1)S(1)}, bf16[4,96,768]{2,1,0:T(8,128)(2,1)S(1)}, u32[]{:S(2)}, u32[]{:S(2)}) %collective-permute-start.39) | collective-permute-done | bytes 589856 | tf_op jit(solution)/shard_map/ppermute | solution.py:490
  214.8 4.3 %collective-permute-done.44 = bf16[2,96,1536]{2,1,0:T(8,128)(2,1)S(1)} collective-permute-done((bf16[2,96,1536]{2,1,0:T(8,128)(2,1)S(1)}, bf16[2,96,1536]{2,1,0:T(8,128)(2,1)S(1)}, u32[]{:S(2)}, u32[]{:S(2)}) %collective-permute-start.44) | collective-permute-done | bytes 589856 | tf_op jit(solution)/shard_map/ppermute | solution.py:493
  219.6 5.8 %collective-permute-done.43 = bf16[2,96,768]{2,1,0:T(8,128)(2,1)S(1)} collective-permute-done((bf16[2,96,768]{2,1,0:T(8,128)(2,1)S(1)}, bf16[2,96,768]{2,1,0:T(8,128)(2,1)S(1)}, u32[]{:S(2)}, u32[]{:S(2)}) %collective-permute-start.43) | collective-permute-done | bytes 294944 | tf_op jit(solution)/shard_map/ppermute | solution.py:493
  229.4 8.2 %collective-permute-done.49 = bf16[1,96,1536]{2,1,0:T(8,128)(2,1)S(1)} collective-permute-done((bf16[1,96,1536]{2,1,0:T(8,128)(2,1)S(1)}, bf16[1,96,1536]{2,1,0:T(8,128)(2,1)S(1)}, u32[]{:S(2)}, u32[]{:S(2)}) %collective-permute-start.49) | collective-permute-done | bytes 294944 | tf_op jit(solution)/shard_map/ppermute | solution.py:493
  238.5 7.5 %collective-permute-done.51 = bf16[2,96,768]{2,1,0:T(8,128)(2,1)S(1)} collective-permute-done((bf16[2,96,768]{2,1,0:T(8,128)(2,1)S(1)}, bf16[2,96,768]{2,1,0:T(8,128)(2,1)S(1)}, u32[]{:S(2)}, u32[]{:S(2)}) %collective-permute-start.51) | collective-permute-done | bytes 294944 | tf_op jit(solution)/shard_map/ppermute | solution.py:493
  246.8 9.5 %collective-permute-done.52 = bf16[1,96,768]{2,1,0:T(8,128)(2,1)S(1)} collective-permute-done((bf16[1,96,768]{2,1,0:T(8,128)(2,1)S(1)}, bf16[1,96,768]{2,1,0:T(8,128)(2,1)S(1)}, u32[]{:S(2)}, u32[]{:S(2)}) %collective-permute-start.52) | collective-permute-done | bytes 147488 | tf_op jit(solution)/shard_map/ppermute | solution.py:493
  (247 shorter events, 104.6 us)
Async XLA Ops:
  8.3 15.5 %collective-permute-start.1 = (bf16[96,1536]{1,0:T(8,128)(2,1)S(1)}, bf16[96,1536]{1,0:T(8,128)(2,1)S(1)}, u32[]{:S(2)}, u32[]{:S(2)}) collective-permute-start(bf16[96,1536]{1,0:T(8,128)(2,1)S(1)} %bitcast_dynamic-update-slice_fusion.1.refs_0_), channel_id=1, source_target_pairs={{0,4},{1,5},{2,6},{3,7},{4,0},{5,1},{6,2},{7,3},{8,12},{9,13},{10,... | collective-permute-start | bytes 884744 | tf_op jit(solution)/shard_map/ppermute | solution.py:493
  24.2 16.5 %collective-permute-start.8 = (bf16[208,768]{1,0:T(8,128)(2,1)S(1)}, bf16[208,768]{1,0:T(8,128)(2,1)S(1)}, u32[]{:S(2)}, u32[]{:S(2)}) collective-permute-start(bf16[208,768]{1,0:T(8,128)(2,1)S(1)} %fusion.9.refs_0_), channel_id=1, source_target_pairs={{0,4},{1,5},{2,6},{3,7},{4,0},{5,1},{6,2},{7,3},{8,12},{9,13},{10,... | collective-permute-start | bytes 958472 | tf_op jit(solution)/shard_map/ppermute | solution.py:493
  45.2 57.3 %collective-permute-start.23 = (bf16[8,96,1536]{2,1,0:T(8,128)(2,1)}, bf16[8,96,1536]{2,1,0:T(8,128)(2,1)}, u32[]{:S(2)}, u32[]{:S(2)}) collective-permute-start(bf16[8,96,1536]{2,1,0:T(8,128)(2,1)} %shard_map.344.mine_ref), channel_id=1, source_target_pairs={{0,16},{8,24},{16,0},{24,8},{1,17},{9,25},{17,1},{25,9},{2,18},{10... | collective-permute-start | bytes 7077896 | tf_op jit(solution)/shard_map/ppermute | solution.py:487
  48.0 15.7 %collective-permute-start.14 = (bf16[208,768]{1,0:T(8,128)(2,1)S(1)}, bf16[208,768]{1,0:T(8,128)(2,1)S(1)}, u32[]{:S(2)}, u32[]{:S(2)}) collective-permute-start(bf16[208,768]{1,0:T(8,128)(2,1)S(1)} %collective-permute-done.8.refs_4_), channel_id=1, source_target_pairs={{0,2},{1,3},{2,0},{3,1},{4,6},{5,7},{6,4},{7,5},{8,10},{9,11},{10,... | collective-permute-start | bytes 958472 | tf_op jit(solution)/shard_map/ppermute | solution.py:493
  64.1 20.3 %collective-permute-start.13 = (bf16[208,768]{1,0:T(8,128)(2,1)S(1)}, bf16[208,768]{1,0:T(8,128)(2,1)S(1)}, u32[]{:S(2)}, u32[]{:S(2)}) collective-permute-start(bf16[208,768]{1,0:T(8,128)(2,1)S(1)} %collective-permute-done.8.refs_4_), channel_id=1, source_target_pairs={{0,1},{1,0},{2,3},{3,2},{4,5},{5,4},{6,7},{7,6},{8,9},{9,8},{10,11... | collective-permute-start | bytes 958472 | tf_op jit(solution)/shard_map/ppermute | solution.py:490
  80.6 15.4 %collective-permute-start.21 = (bf16[192,768]{1,0:T(8,128)(2,1)S(1)}, bf16[192,768]{1,0:T(8,128)(2,1)S(1)}, u32[]{:S(2)}, u32[]{:S(2)}) collective-permute-start(bf16[192,768]{1,0:T(8,128)(2,1)S(1)} %collective-permute-done.18.refs_6_), channel_id=1, source_target_pairs={{0,1},{1,0},{2,3},{3,2},{4,5},{5,4},{6,7},{7,6},{8,9},{9,8},{10,11... | collective-permute-start | bytes 884744 | tf_op jit(solution)/shard_map/ppermute | solution.py:490
  87.1 18.6 %collective-permute-start.17 = (bf16[8,208,768]{2,1,0:T(8,128)(2,1)S(1)}, bf16[8,208,768]{2,1,0:T(8,128)(2,1)}, u32[]{:S(2)}, u32[]{:S(2)}) collective-permute-start(bf16[8,208,768]{2,1,0:T(8,128)(2,1)S(1)} %shard_map.340.mine), channel_id=1, source_target_pairs={{0,8},{8,0},{16,24},{24,16},{1,9},{9,1},{17,25},{25,17},{2,10},{10... | collective-permute-start | bytes 7667720 | tf_op jit(solution)/shard_map/ppermute | solution.py:487
  102.5 25.5 %collective-permute-start.24 = (bf16[8,96,1536]{2,1,0:T(8,128)(2,1)}, bf16[8,96,1536]{2,1,0:T(8,128)(2,1)}, u32[]{:S(2)}, u32[]{:S(2)}) collective-permute-start(bf16[8,96,1536]{2,1,0:T(8,128)(2,1)} %collective-permute-done.23.mine_ref), channel_id=1, source_target_pairs={{0,8},{8,0},{16,24},{24,16},{1,9},{9,1},{17,25},{25,17},{2,10},{10... | collective-permute-start | bytes 7077896 | tf_op jit(solution)/shard_map/ppermute | solution.py:487
  141.7 29.1 %collective-permute-start.31 = (bf16[4,96,1536]{2,1,0:T(8,128)(2,1)}, bf16[4,96,1536]{2,1,0:T(8,128)(2,1)}, u32[]{:S(2)}, u32[]{:S(2)}) collective-permute-start(bf16[4,96,1536]{2,1,0:T(8,128)(2,1)} %fusion.2), channel_id=1, source_target_pairs={{0,1},{1,0},{2,3},{3,2},{4,5},{5,4},{6,7},{7,6},{8,9},{9,8},{10,11... | collective-permute-start | bytes 3538952 | tf_op jit(solution)/shard_map/ppermute | solution.py:490
  152.6 25.9 %collective-permute-start.33 = (bf16[8,96,768]{2,1,0:T(8,128)(2,1)}, bf16[8,96,768]{2,1,0:T(8,128)(2,1)}, u32[]{:S(2)}, u32[]{:S(2)}) collective-permute-start(bf16[8,96,768]{2,1,0:T(8,128)(2,1)} %get-tuple-element.194), channel_id=1, source_target_pairs={{0,8},{8,0},{16,24},{24,16},{1,9},{9,1},{17,25},{25,17},{2,10},{10... | collective-permute-start | bytes 3538952 | tf_op jit(solution)/shard_map/ppermute | solution.py:487
  155.4 40.7 %collective-permute-start.36 = (bf16[4,96,1536]{2,1,0:T(8,128)(2,1)}, bf16[4,96,1536]{2,1,0:T(8,128)(2,1)}, u32[]{:S(2)}, u32[]{:S(2)}) collective-permute-start(bf16[4,96,1536]{2,1,0:T(8,128)(2,1)} %fusion.3), channel_id=1, source_target_pairs={{0,1},{1,0},{2,3},{3,2},{4,5},{5,4},{6,7},{7,6},{8,9},{9,8},{10,11... | collective-permute-start | bytes 3538952 | tf_op jit(solution)/shard_map/ppermute | solution.py:490
  158.5 29.1 %collective-permute-start.34 = (bf16[8,96,768]{2,1,0:T(8,128)(2,1)}, bf16[8,96,768]{2,1,0:T(8,128)(2,1)}, u32[]{:S(2)}, u32[]{:S(2)}) collective-permute-start(bf16[8,96,768]{2,1,0:T(8,128)(2,1)} %add_convert_fusion.1), channel_id=1, source_target_pairs={{0,16},{8,24},{16,0},{24,8},{1,17},{9,25},{17,1},{25,9},{2,18},{10... | collective-permute-start | bytes 3538952 | tf_op jit(solution)/shard_map/ppermute | solution.py:487
  174.4 15.6 %collective-permute-start.37 = (bf16[2,96,1536]{2,1,0:T(8,128)(2,1)}, bf16[2,96,1536]{2,1,0:T(8,128)(2,1)}, u32[]{:S(2)}, u32[]{:S(2)}) collective-permute-start(bf16[2,96,1536]{2,1,0:T(8,128)(2,1)} %pad_maximum_fusion), channel_id=1, source_target_pairs={{0,2},{1,3},{2,0},{3,1},{4,6},{5,7},{6,4},{7,5},{8,10},{9,11},{10,... | collective-permute-start | bytes 1769480 | tf_op jit(solution)/shard_map/ppermute | solution.py:493
  176.4 33.9 %collective-permute-start.40 = (bf16[8,96,768]{2,1,0:T(8,128)(2,1)}, bf16[8,96,768]{2,1,0:T(8,128)(2,1)S(1)}, u32[]{:S(2)}, u32[]{:S(2)}) collective-permute-start(bf16[8,96,768]{2,1,0:T(8,128)(2,1)} %get-tuple-element.203), channel_id=1, source_target_pairs={{0,8},{8,0},{16,24},{24,16},{1,9},{9,1},{17,25},{25,17},{2,10},{10... | collective-permute-start | bytes 3538952 | tf_op jit(solution)/shard_map/ppermute | solution.py:487
  178.5 33.6 %collective-permute-start.41 = (bf16[8,96,768]{2,1,0:T(8,128)(2,1)S(1)}, bf16[8,96,768]{2,1,0:T(8,128)(2,1)S(1)}, u32[]{:S(2)}, u32[]{:S(2)}) collective-permute-start(bf16[8,96,768]{2,1,0:T(8,128)(2,1)S(1)} %add_convert_fusion), channel_id=1, source_target_pairs={{0,16},{8,24},{16,0},{24,8},{1,17},{9,25},{17,1},{25,9},{2,18},{10... | collective-permute-start | bytes 3538952 | tf_op jit(solution)/shard_map/ppermute | solution.py:487
  189.1 19.1 %collective-permute-start.39 = (bf16[4,96,768]{2,1,0:T(8,128)(2,1)S(1)}, bf16[4,96,768]{2,1,0:T(8,128)(2,1)S(1)}, u32[]{:S(2)}, u32[]{:S(2)}) collective-permute-start(bf16[4,96,768]{2,1,0:T(8,128)(2,1)S(1)} %fusion.7), channel_id=1, source_target_pairs={{0,1},{1,0},{2,3},{3,2},{4,5},{5,4},{6,7},{7,6},{8,9},{9,8},{10,11... | collective-permute-start | bytes 1769480 | tf_op jit(solution)/shard_map/ppermute | solution.py:490
  191.0 22.0 %collective-permute-start.45 = (bf16[1,96,1536]{2,1,0:T(8,128)(2,1)S(1)}, bf16[1,96,1536]{2,1,0:T(8,128)(2,1)S(1)}, u32[]{:S(2)}, u32[]{:S(2)}) collective-permute-start(bf16[1,96,1536]{2,1,0:T(8,128)(2,1)S(1)} %add_convert_fusion.13), channel_id=1, source_target_pairs={{0,4},{1,5},{2,6},{3,7},{4,0},{5,1},{6,2},{7,3},{8,12},{9,13},{10,... | collective-permute-start | bytes 884744 | tf_op jit(solution)/shard_map/ppermute | solution.py:493
  199.5 19.6 %collective-permute-start.44 = (bf16[2,96,1536]{2,1,0:T(8,128)(2,1)S(1)}, bf16[2,96,1536]{2,1,0:T(8,128)(2,1)S(1)}, u32[]{:S(2)}, u32[]{:S(2)}) collective-permute-start(bf16[2,96,1536]{2,1,0:T(8,128)(2,1)S(1)} %pad_maximum_fusion.1), channel_id=1, source_target_pairs={{0,2},{1,3},{2,0},{3,1},{4,6},{5,7},{6,4},{7,5},{8,10},{9,11},{10,... | collective-permute-start | bytes 1769480 | tf_op jit(solution)/shard_map/ppermute | solution.py:493
  214.1 23.5 %collective-permute-start.50 = (bf16[96,1536]{1,0:T(8,128)(2,1)S(1)}, bf16[96,1536]{1,0:T(8,128)(2,1)S(1)}, u32[]{:S(2)}, u32[]{:S(2)}) collective-permute-start(bf16[96,1536]{1,0:T(8,128)(2,1)S(1)} %fusion.10), channel_id=1, source_target_pairs={{0,16},{8,24},{16,0},{24,8},{1,17},{9,25},{17,1},{25,9},{2,18},{10... | collective-permute-start | bytes 884744 | tf_op jit(solution)/shard_map/ppermute | solution.py:487
  219.1 18.5 %collective-permute-start.49 = (bf16[1,96,1536]{2,1,0:T(8,128)(2,1)S(1)}, bf16[1,96,1536]{2,1,0:T(8,128)(2,1)S(1)}, u32[]{:S(2)}, u32[]{:S(2)}) collective-permute-start(bf16[1,96,1536]{2,1,0:T(8,128)(2,1)S(1)} %add_convert_fusion.11), channel_id=1, source_target_pairs={{0,4},{1,5},{2,6},{3,7},{4,0},{5,1},{6,2},{7,3},{8,12},{9,13},{10,... | collective-permute-start | bytes 884744 | tf_op jit(solution)/shard_map/ppermute | solution.py:493
  225.4 20.6 %collective-permute-start.56 = (bf16[1,96,768]{2,1,0:T(8,128)(2,1)S(1)}, bf16[1,96,768]{2,1,0:T(8,128)(2,1)S(1)}, u32[]{:S(2)}, u32[]{:S(2)}) collective-permute-start(bf16[1,96,768]{2,1,0:T(8,128)(2,1)S(1)} %add_convert_fusion.19), channel_id=1, source_target_pairs={{0,4},{1,5},{2,6},{3,7},{4,0},{5,1},{6,2},{7,3},{8,12},{9,13},{10,... | collective-permute-start | bytes 442376 | tf_op jit(solution)/shard_map/ppermute | solution.py:493
  227.7 18.2 %collective-permute-start.51 = (bf16[2,96,768]{2,1,0:T(8,128)(2,1)S(1)}, bf16[2,96,768]{2,1,0:T(8,128)(2,1)S(1)}, u32[]{:S(2)}, u32[]{:S(2)}) collective-permute-start(bf16[2,96,768]{2,1,0:T(8,128)(2,1)S(1)} %pad_maximum_fusion.4), channel_id=1, source_target_pairs={{0,2},{1,3},{2,0},{3,1},{4,6},{5,7},{6,4},{7,5},{8,10},{9,11},{10,... | collective-permute-start | bytes 884744 | tf_op jit(solution)/shard_map/ppermute | solution.py:493
  238.4 22.6 %collective-permute-start.58 = (bf16[96,1536]{1,0:T(8,128)(2,1)S(1)}, bf16[96,1536]{1,0:T(8,128)(2,1)S(1)}, u32[]{:S(2)}, u32[]{:S(2)}) collective-permute-start(bf16[96,1536]{1,0:T(8,128)(2,1)S(1)} %get-tuple-element.232.two), channel_id=1, source_target_pairs={{0,8},{8,0},{16,24},{24,16},{1,9},{9,1},{17,25},{25,17},{2,10},{10... | collective-permute-start | bytes 884744 | tf_op jit(solution)/shard_map/ppermute | solution.py:487
  238.4 18.5 %collective-permute-start.48 = (f32[4,768]{1,0:T(4,128)S(1)}, f32[4,768]{1,0:T(4,128)S(1)}, u32[]{:S(2)}, u32[]{:S(2)}) collective-permute-start(f32[4,768]{1,0:T(4,128)S(1)} %add.248), channel_id=1, source_target_pairs={{0,4},{1,5},{2,6},{3,7},{4,0},{5,1},{6,2},{7,3},{8,12},{9,13},{10,... | collective-permute-start | bytes 36872 | tf_op jit(solution)/shard_map/ppermute | solution.py:824
  (71 other events, 767.8 us)
